TPU v7x, 256 devices: a whole 4x4x8 slice. The times are simulated.
256 devices in a mesh: rep: 8 (over y, core), fsdp: 32 (over z, x).
Axes of the slice: x: 4, y: 4, z: 8, core: 2. Of those that a mesh axis runs over, the one named last changes fastest.
Arguments:
- tokens: bfloat16 [147456, 512], P(('rep', 'fsdp')), may hold values from -6 to 6
- cotangent: bfloat16 [147456, 512], P(('rep', 'fsdp')), may hold values from -6 to 6
- window_order: int32 [256, 576], P(('rep', 'fsdp')), may hold values from 0 to 575, each once within a row
- gain: float32 [512], replicated, may hold values from 0.1 to 1.9
- w_qkv: bfloat16 [512, 1536], P('fsdp'), may hold values from -8 to 8
- w_out: bfloat16 [512, 512], P('fsdp'), may hold values from -0.25 to 0.25
- err_qkv: float32 [8, 512, 1536], P('rep', 'fsdp'), may hold values from -6 to 6
- err_out: float32 [8, 512, 512], P('rep', 'fsdp'), may hold values from -6 to 6
- q_qkv: int32 [1536, 32], replicated, may hold values from -127 to 127
- q_out: int32 [512, 32], replicated, may hold values from -127 to 127
Outputs:
- d_tokens: bfloat16 [147456, 512], P(('rep', 'fsdp'))
- grad_qkv: float32 [512, 1536], P('fsdp')
- grad_out: float32 [512, 512], P('fsdp')
- err_qkv_next: float32 [8, 512, 1536], P('rep', 'fsdp')
- err_out_next: float32 [8, 512, 512], P('rep', 'fsdp')
- basis_qkv_next: float32 [1536, 32], replicated
- basis_out_next: float32 [512, 32], replicated
Inputs may be any that keep to these rules, and one draw needn't show every extreme that they name: `window_order`: each row is a permutation of 0 to 575.
All inputs are finite; a program needn't handle non-finite values.
Results may differ from a plain program's by a relative error of at most 0.017.
Values may be sent and summed in bfloat16 or wider, within the bound.
A program may use at most 64 MiB of HBM per device.

v0:
```python
import jax
import jax.numpy as jnp
from jax import lax
from jax.sharding import PartitionSpec as P

HEADS = 8
WT = 144


def layer_norm(values, gain):
    center = values - jnp.mean(values, -1, keepdims=True)
    spread = jnp.mean(center * center, -1, keepdims=True)
    return (center * lax.rsqrt(spread + 1e-05) * gain).astype(jnp.bfloat16)


def attend(qkv, heads):
    count, span, triple = qkv.shape
    width = triple // 3
    size = width // heads
    parts = qkv.reshape(count, span, 3, heads, size).astype(jnp.float32)
    query = parts[:, :, 0]
    key_part = parts[:, :, 1]
    value = parts[:, :, 2]
    scores = jnp.einsum("nqhd,nkhd->nhqk", query, key_part) * size ** (-0.5)
    top = jnp.max(scores, -1, keepdims=True)
    weights = jnp.exp(scores - top)
    weights = weights / jnp.sum(weights, -1, keepdims=True)
    probs = lax.optimization_barrier(weights.astype(jnp.bfloat16)).astype(jnp.float32)
    context = jnp.einsum("nhqk,nkhd->nqhd", probs, value)
    return context.astype(jnp.bfloat16).reshape(count, span, width)


def times_transposed(left, piece):
    return lax.dot_general(
        left, piece, (((1,), (1,)), ((), ())), preferred_element_type=jnp.float32
    )


def first_transposed(left, right):
    return lax.dot_general(
        left,
        right,
        (((0,), (0,)), ((), ())),
        precision=lax.Precision.HIGHEST,
        preferred_element_type=jnp.float32,
    )


def orthonormal(left, gram):
    lower = jnp.linalg.cholesky(gram)
    return jax.scipy.linalg.solve_triangular(lower, left.T, lower=True).T


def per_device(tokens, cotangent, window_order, gain, w_qkv, w_out, err_qkv, err_out, q_qkv, q_out):
    highest = lax.Precision.HIGHEST
    order = window_order[0]
    rows = jnp.take(tokens, order, axis=0)
    back = jnp.take(cotangent, order, axis=0)
    width = tokens.shape[1]
    local_rows = rows.shape[0]
    scale = float(lax.axis_size("fsdp") * local_rows) ** (-0.5)
    replicas = lax.axis_size("rep")
    normed, norm_back = jax.vjp(lambda v: layer_norm(v, gain), rows.astype(jnp.float32))
    columns = normed
    qkv = jnp.dot(
        columns,
        lax.all_gather(w_qkv, "fsdp", axis=0, tiled=True),
        preferred_element_type=jnp.float32,
    ).astype(jnp.bfloat16)
    context, attend_back = jax.vjp(
        lambda a: attend(a.reshape(-1, WT, 3 * width), HEADS).reshape(-1, width), qkv
    )
    columns = context
    g_out = lax.psum_scatter(
        (
            lax.dot_general(
                columns, back, (((0,), (0,)), ((), ())), preferred_element_type=jnp.float32
            )
            * scale
        ).astype(jnp.bfloat16),
        "fsdp",
        scatter_dimension=0,
        tiled=True,
    ).astype(jnp.float32)
    d_context = times_transposed(back, lax.all_gather(w_out, "fsdp", axis=0, tiled=True)).astype(
        jnp.bfloat16
    )
    d_qkv = attend_back(d_context)[0]
    columns = normed
    g_qkv = lax.psum_scatter(
        (
            lax.dot_general(
                columns, d_qkv, (((0,), (0,)), ((), ())), preferred_element_type=jnp.float32
            )
            * scale
        ).astype(jnp.bfloat16),
        "fsdp",
        scatter_dimension=0,
        tiled=True,
    ).astype(jnp.float32)
    d_normed = times_transposed(d_qkv, lax.all_gather(w_qkv, "fsdp", axis=0, tiled=True)).astype(
        jnp.bfloat16
    )
    d_rows = norm_back(d_normed)[0]
    d_win = (back.astype(jnp.float32) + d_rows).astype(jnp.bfloat16)
    d_tokens = jnp.zeros_like(tokens).at[order].set(d_win)
    basis_qkv = q_qkv.astype(jnp.float32) / 127.0
    basis_out = q_out.astype(jnp.float32) / 127.0
    total_qkv = g_qkv + err_qkv[0]
    total_out = g_out + err_out[0]
    left_qkv = jnp.dot(total_qkv, basis_qkv, precision=highest)
    left_out = jnp.dot(total_out, basis_out, precision=highest)
    left_qkv, left_out = lax.psum((left_qkv, left_out), "rep")
    left_qkv = left_qkv / replicas
    left_out = left_out / replicas
    gram_qkv, gram_out = lax.psum(
        (
            jnp.dot(left_qkv.T, left_qkv, precision=highest),
            jnp.dot(left_out.T, left_out, precision=highest),
        ),
        "fsdp",
    )
    ortho_qkv = orthonormal(left_qkv, gram_qkv)
    ortho_out = orthonormal(left_out, gram_out)
    right_qkv = first_transposed(total_qkv, ortho_qkv)
    right_out = first_transposed(total_out, ortho_out)
    right_qkv, right_out = lax.psum((right_qkv, right_out), ("rep", "fsdp"))
    right_qkv = right_qkv / replicas
    right_out = right_out / replicas
    grad_qkv = jnp.dot(ortho_qkv, right_qkv.T, precision=highest)
    grad_out = jnp.dot(ortho_out, right_out.T, precision=highest)
    return (
        d_tokens,
        grad_qkv,
        grad_out,
        (total_qkv - grad_qkv)[None],
        (total_out - grad_out)[None],
        right_qkv,
        right_out,
    )


def solution(mesh):
    return jax.shard_map(
        per_device,
        mesh=mesh,
        in_specs=(
            P(("rep", "fsdp"), None),
            P(("rep", "fsdp"), None),
            P(("rep", "fsdp"), None),
            P(),
            P("fsdp", None),
            P("fsdp", None),
            P("rep", "fsdp", None),
            P("rep", "fsdp", None),
            P(),
            P(),
        ),
        out_specs=(
            P(("rep", "fsdp"), None),
            P("fsdp", None),
            P("fsdp", None),
            P("rep", "fsdp", None),
            P("rep", "fsdp", None),
            P(),
            P(),
        ),
        check_vma=False,
    )
```

profile of v0, /device:TPU:1, one launch (start us, length us, event | category | flops | bytes accessed | tf_op | source)
XLA Modules:
  0.0 994.2 jit_solution(16227934700687965174)
XLA Ops:
  8.7 2.7 gather_fusion.1
  11.5 2.7 gather_fusion
  14.3 43.1 %all_gather.7 = bf16[512,512]{1,0:T(8,128)(2,1)S(1)} all-gather(bf16[16,512]{1,0:T(8,128)(2,1)S(1)} %copy-done.28), channel_id=1, replica_groups=mesh['rep'=8,'fsdp'=32] {'fsdp'}, dimensions={0}, use_global_device_ids=true | all-gather | bytes 540672 | tf_op jit(solution)/shard_map/all_gather | solution.py:85
  58.2 1.7 reshape.108
  60.7 26.7 %all-gather.2.cloned.1.call-done = bf16[512,1536]{1,0:T(8,128)(2,1)} async-done(((bf16[16,1536]{1,0:T(8,128)(2,1)}), bf16[512,1536]{1,0:T(8,128)(2,1)}) %all-gather.2.cloned.1.call-update) | async-done | bytes 1572880 | tf_op jit(solution)/shard_map/all_gather | solution.py:67
  87.3 2.6 convolution_convert_fusion
  89.9 3.6 reshape.142
  93.5 3.2 fusion.88
  96.8 2.6 copy.59
  102.5 2.5 convolution_convert_fusion.1
  106.9 1.7 fusion.3
  108.7 4.6 divide_convert_fusion
  115.2 1.8 copy.45
  117.0 3.0 reshape.111
  120.0 2.8 fusion.23
  123.9 5.4 fusion.14
  129.3 2.5 fusion.15
  133.2 4.5 copy.41
  137.8 5.4 reshape.110
  143.2 2.9 fusion.6
  146.5 3.5 fusion.27
  150.5 182.1 %reduce-scatter.5.cloned.1.call-done = bf16[16,512]{1,0:T(8,128)(2,1)} async-done(((bf16[512,512]{1,0:T(8,128)(2,1)}), bf16[16,512]{1,0:T(8,128)(2,1)}) %reduce-scatter.5.cloned.1.call-update) | async-done | bytes 16400 | tf_op jit(solution)/shard_map/reduce_scatter | solution.py:74
  333.5 218.0 %reduce-scatter.3.cloned.1.call-done = bf16[16,1536]{1,0:T(8,128)(2,1)} async-done(((bf16[512,1536]{1,0:T(8,128)(2,1)}), bf16[16,1536]{1,0:T(8,128)(2,1)}) %reduce-scatter.3.cloned.1.call-update) | async-done | bytes 49168 | tf_op jit(solution)/shard_map/reduce_scatter | solution.py:90
  552.5 26.2 %all-reduce.5 = (f32[16,32]{1,0:T(8,128)S(1)}, f32[16,32]{1,0:T(8,128)S(1)}) all-reduce(f32[16,32]{1,0:T(8,128)S(1)} %fusion.40, f32[16,32]{1,0:T(8,128)S(1)} %fusion.44), channel_id=1, replica_groups=mesh['rep'=8,'fsdp'=32] {'rep'}, use_global_device_ids=true, to_apply=%region_11.13 | all-reduce | flops 1024 | bytes 8192 | tf_op jit(solution)/shard_map/psum | solution.py:113
  579.1 112.7 %all-reduce.4 = (f32[32,32]{0,1:T(8,128)S(1)}, f32[32,32]{0,1:T(8,128)S(1)}) all-reduce(f32[32,32]{0,1:T(8,128)S(1)} %fusion.64, f32[32,32]{0,1:T(8,128)S(1)} %fusion.61), channel_id=1, replica_groups=mesh['rep'=8,'fsdp'=32] {'fsdp'}, use_global_device_ids=true, to_apply=%region_12.14 | all-reduce | flops 2048 | bytes 16384 | tf_op jit(solution)/shard_map/psum | solution.py:116
  692.0 2.9 cholesky.55
  696.3 2.4 custom-call.7
  698.9 2.9 cholesky.44
  703.1 2.4 custom-call.6
  707.3 1.8 fusion.47
  709.2 7.6 scatter_custom_fusion
  716.8 267.2 %all-reduce.8.cloned.1.call-done = (f32[1536,32]{0,1:T(8,128)}, f32[512,32]{0,1:T(8,128)}) async-done(((f32[1536,32]{0,1:T(8,128)}, f32[512,32]{0,1:T(8,128)}), (f32[1536,32]{0,1:T(8,128)}, f32[512,32]{0,1:T(8,128)})) %all-reduce.8.cloned.1.call-update) | async-done | bytes 262160 | tf_op jit(solution)/shard_map/psum | solution.py:127
  (123 shorter events, 24.1 us)
Async XLA Ops:
  7.2 80.1 %all-gather.2.cloned.1.call-start = ((), (), s32[]{:S(2)}) async-start(), calls=%async_computation.2 | async-start | bytes 1622016 | tf_op jit(solution)/shard_map/all_gather | solution.py:67
  7.9 324.7 %reduce-scatter.5.cloned.1.call-start = ((), (), s32[]{:S(2)}) async-start(), calls=%async_computation.4 | async-start | bytes 540672 | tf_op jit(solution)/shard_map/reduce_scatter | solution.py:74
  8.7 2.8 copy-start.2
  11.5 75.8 %copy-start.5 = (bf16[576,512]{1,0:T(8,128)(2,1)}, bf16[576,512]{1,0:T(8,128)(2,1)S(1)}, u32[]{:S(2)}) copy-start(bf16[576,512]{1,0:T(8,128)(2,1)S(1)} %gather_fusion.1) | copy-start | bytes 1769476
  11.5 2.8 copy-start.28
  14.3 43.1 %copy-start.12 = (bf16[576,512]{1,0:T(8,128)(2,1)}, bf16[576,512]{1,0:T(8,128)(2,1)S(1)}, u32[]{:S(2)}) copy-start(bf16[576,512]{1,0:T(8,128)(2,1)S(1)} %gather_fusion) | copy-start | bytes 1769476
  58.2 29.1 %copy-start.30 = (f32[512]{0:T(512)S(1)}, f32[512]{0:T(512)}, u32[]{:S(2)}) copy-start(f32[512]{0:T(512)} %param.18) | copy-start | bytes 6148
  102.5 2.5 copy-start.9
  102.5 2.5 copy-start.11
  106.0 2.7 copy-start.1
  108.6 4.6 copy-start.24
  108.7 6.0 copy-start.7
  122.8 6.5 slice-start
  122.8 428.7 %reduce-scatter.3.cloned.1.call-start = ((), (), s32[]{:S(2)}) async-start(), calls=%async_computation.3 | async-start | bytes 1622016 | tf_op jit(solution)/shard_map/reduce_scatter | solution.py:90
  123.8 5.4 slice-start.1
  123.8 5.4 copy-start.10
  123.9 5.4 copy-start.15
  123.9 5.4 copy-start.25
  129.3 2.5 copy-start.4
  137.7 5.4 copy-start.6
  137.8 5.4 copy-start.31
  143.2 2.9 copy-start.14
  143.2 3.2 copy-start.29
  146.1 837.9 %all-reduce.8.cloned.1.call-start = ((), (), s32[]{:S(2)}) async-start(), calls=%async_computation.5 | async-start | bytes 524288 | tf_op jit(solution)/shard_map/psum | solution.py:127
  146.4 186.2 %copy-start.20 = (f32[1,16,512]{2,1,0:T(8,128)S(1)}, f32[1,16,512]{2,1,0:T(8,128)}, u32[]{:S(2)}) copy-start(f32[1,16,512]{2,1,0:T(8,128)} %param.22) | copy-start | bytes 98308
  146.5 186.2 %copy-start.27 = (s32[512,32]{0,1:T(8,128)S(1)}, s32[512,32]{0,1:T(8,128)}, u32[]{:S(2)}) copy-start(s32[512,32]{0,1:T(8,128)} %param.24) | copy-start | bytes 196612
  146.5 405.0 %copy-start.16 = (f32[1,16,1536]{2,1,0:T(8,128)S(1)}, f32[1,16,1536]{2,1,0:T(8,128)}, u32[]{:S(2)}) copy-start(f32[1,16,1536]{2,1,0:T(8,128)} %param.21) | copy-start | bytes 294916
  146.5 405.0 %copy-start.22 = (s32[1536,32]{0,1:T(8,128)S(1)}, s32[1536,32]{0,1:T(8,128)}, u32[]{:S(2)}) copy-start(s32[1536,32]{0,1:T(8,128)} %param.23) | copy-start | bytes 589828
  150.0 559.2 %copy-start.13 = (bf16[576,512]{1,0:T(8,128)(2,1)S(1)}, bf16[576,512]{1,0:T(8,128)(2,1)}, u32[]{:S(2)}) copy-start(bf16[576,512]{1,0:T(8,128)(2,1)} %copy-done.12) | copy-start | bytes 1769476
  702.5 283.8 %copy-start.23 = (bf16[16,512]{1,0:T(8,128)(2,1)S(1)}, bf16[16,512]{1,0:T(8,128)(2,1)}, u32[]{:S(2)}) copy-start(bf16[16,512]{1,0:T(8,128)(2,1)} %reduce-scatter.5.cloned.1.call-done) | copy-start | bytes 49156
  705.7 281.2 %copy-start.18 = (bf16[16,1536]{1,0:T(8,128)(2,1)S(1)}, bf16[16,1536]{1,0:T(8,128)(2,1)}, u32[]{:S(2)}) copy-start(bf16[16,1536]{1,0:T(8,128)(2,1)} %reduce-scatter.3.cloned.1.call-done) | copy-start | bytes 147460
  985.0 2.7 copy-start.17
  (6 other events, 10.1 us)
Sparse Core Ops, SparseCore 0:
  10.6 76.6 all-gather.1
  122.9 209.6 reduce-scatter.4
  336.9 214.5 reduce-scatter.2
  709.3 274.6 all-reduce.7
where the time goes:
time: 996 us; the launch traced here: 994 us
  waiting for transfers between devices  695 us (70%)
  blocking collectives  182 us (18%)
  local copies, waits for them, and re-layouts  36.5 us (4%)
  other arithmetic  34.6 us (3%)
  matrix products  31.4 us (3%)
  between operations  14.4 us (1%)
    psum x1, waiting for transfers between devices, per_device(): right_qkv, right_out = lax.psum((right_qkv, right_out), ('rep', 'fsdp'))  267 us
    reduce_scatter x1, waiting for transfers between devices, per_device(): lax.psum_scatter((lax.dot_general(columns, d_qkv, (((0,), (0,)), ((), ())...  218 us
    reduce_scatter x1, waiting for transfers between devices, per_device(): lax.psum_scatter((lax.dot_general(columns, back, (((0,), (0,)), ((), ()))...  182 us
    psum x1, blocking collectives, per_device(): lax.psum((jnp.dot(left_qkv.T, left_qkv, precision=highest), jnp.dot(left_...  113 us
    all_gather x1, blocking collectives, per_device(): lax.all_gather(w_out, 'fsdp', axis=0, tiled=True)  43.1 us
    all_gather x1, waiting for transfers between devices, per_device(): lax.all_gather(w_qkv, 'fsdp', axis=0, tiled=True)  26.7 us
    psum x1, blocking collectives, per_device(): left_qkv, left_out = lax.psum((left_qkv, left_out), 'rep')  26.2 us
  transfers between devices with their start and end apart: 4, of which 4 were waited for; matrix products, arithmetic and copies ran while one was open for 5% of the time, Pallas kernels for 0%

commit v1 on v0

v1 whole, which is shorter than its diff:
```python
import functools

import jax
import jax.numpy as jnp
from jax import lax
from jax.experimental import pallas as pl
from jax.experimental.pallas import tpu as pltpu
from jax.sharding import PartitionSpec as P

f32 = jnp.float32
bf16 = jnp.bfloat16
MESH = pl.DeviceIdType.MESH
HI = lax.Precision.HIGHEST
def dot(a,b): return jnp.dot(a,b,preferred_element_type=f32)
def dnt(a,b): return lax.dot_general(a,b,(((1,),(1,)),((),())),preferred_element_type=f32)
WT=144; NW=4
LOG2E=1.4426950408889634
def front_window(w,order_ref,tok_ref,cot_ref,gain_ref,back_ref,n_ref,xh_ref,rstd_ref):
        row=order_ref[...]
        T=row.shape[1]
        gain=gain_ref[...]
        sl=pl.ds(w*WT,WT)
        si=lax.broadcasted_iota(jnp.int32,(WT,T),0)+w*WT
        li=lax.broadcasted_iota(jnp.int32,(WT,T),1)
        col=jnp.sum(jnp.where(si==li,row,0).astype(f32),axis=1,keepdims=True).astype(jnp.int32)
        oh=jnp.where(col==li,1.0,0.0).astype(bf16)
        x=dot(oh,tok_ref[...])
        back_ref[sl,:]=dot(oh,cot_ref[...]).astype(bf16)
        ce=x-jnp.mean(x,-1,keepdims=True)
        rs=lax.rsqrt(jnp.mean(ce*ce,-1,keepdims=True)+1e-5)
        xh=ce*rs
        xh_ref[sl,:]=xh
        rstd_ref[sl,:]=rs
        n=(xh*gain).astype(bf16)
        n_ref[sl,:]=n
def pair(n_ref,nt_ref,back_ref,W,WO,d_ref,dn_ref,qkvc_ref,scale,first,g_store,go_store,mid=None):
    qkvc_ref[:,:384]=dot(n_ref[...],W).astype(bf16)
    qkvc_ref[:,384:]=dnt(back_ref[...],WO).astype(bf16)
    if mid is not None: mid()
    lane=lax.broadcasted_iota(jnp.int32,(WT,128),1)
    go=jnp.zeros((128,512),f32)
    for w in range(NW):
        sl=pl.ds(w*WT,WT)
        q=qkvc_ref[sl,0:128]; k=qkvc_ref[sl,128:256]; v=qkvc_ref[sl,256:384]; c=qkvc_ref[sl,384:512]
        qt=q.T; kt=k.T; vt=v.T; ct=c.T
        cts=[];dqs=[]
        dv=jnp.zeros((WT,128),f32); dk=jnp.zeros((WT,128),f32)
        for h in range(2):
            m=(lane<64) if h==0 else (lane>=64)
            z=jnp.zeros((),bf16)
            s=dot(jnp.where(m,k,z),qt)
            mx=jnp.max(s,axis=0,keepdims=True)
            e=jnp.exp2((s-mx)*(0.125*LOG2E))
            wt=e*(1.0/jnp.sum(e,axis=0,keepdims=True))
            p=wt.astype(bf16)
            cts.append(dot(vt[64*h:64*h+64],p))
            dp=dot(jnp.where(m,v,z),ct).astype(bf16).astype(f32)
            t=wt*dp
            ds=(t-wt*jnp.sum(t,axis=0,keepdims=True)).astype(bf16)
            dv=dv+dot(p,jnp.where(m,c,z))
            dk=dk+dot(ds,jnp.where(m,q,z))
            dqs.append(dot(kt[64*h:64*h+64],ds))
        ctx=jnp.concatenate(cts,0).astype(bf16)
        go=go+dot(ctx,back_ref[sl,:])
        dq=(jnp.concatenate(dqs,0)*0.125).astype(bf16).T
        d_ref[sl,0:128]=dq
        d_ref[sl,128:256]=(dk*0.125).astype(bf16)
        d_ref[sl,256:384]=dv.astype(bf16)
    go_store((go*scale).astype(bf16))
    g_store((dot(nt_ref[...],d_ref[...])*scale).astype(bf16))
    dn=dnt(d_ref[...],W)
    dn_ref[...]=jnp.where(first,0.0,dn_ref[...])+dn
def tail_norm(dn_ref,xh_ref,rstd_ref,gain_ref,back_ref,dwin_ref):
    gain=gain_ref[...]
    for w in range(NW):
        sl=pl.ds(w*WT,WT)
        dx=dn_ref[sl,:].astype(bf16).astype(f32)*gain
        xh=xh_ref[sl,:]
        d=rstd_ref[sl,:]*(dx-jnp.mean(dx,-1,keepdims=True)-xh*jnp.mean(dx*xh,-1,keepdims=True))
        dwin_ref[sl,:]=(back_ref[sl,:].astype(f32)+d).astype(bf16)

def tail_put(order_ref,dwin_ref,out_ref):
    row=order_ref[...]
    T=row.shape[1]
    for w in range(NW):
        sl=pl.ds(w*WT,WT)
        si=lax.broadcasted_iota(jnp.int32,(WT,T),0)+w*WT
        oh=jnp.where(si==row,1.0,0.0).astype(bf16)
        out_ref[sl,:]=dot(oh,dwin_ref[...]).astype(bf16)


def dnt_hi(a, b):
    return lax.dot_general(a, b, (((1,), (1,)), ((), ())), precision=HI, preferred_element_type=f32)


def remote(src, dst, ss, rs, dev):
    return pltpu.make_async_remote_copy(
        src_ref=src, dst_ref=dst, send_sem=ss, recv_sem=rs, device_id=dev, device_id_type=MESH
    )


def hdot(a, b):
    return jnp.dot(a, b, precision=HI, preferred_element_type=f32)


def split3(v):
    a = v.astype(bf16)
    r = v - a.astype(f32)
    b = r.astype(bf16)
    c = (r - b.astype(f32)).astype(bf16)
    return jnp.concatenate([a, b, c], 0)


def inverse_factors(gram):
    lane = lax.broadcasted_iota(jnp.int32, (32, 128), 1)
    row = lax.broadcasted_iota(jnp.int32, (32, 128), 0)
    first = (lane % 64) < 32
    state = jnp.where(lane < 64, gram, jnp.where((lane % 32) == row, 1.0, 0.0))
    for j in range(31):
        cols = jnp.where(first, state[:, j : j + 1], state[:, 32 + j : 33 + j])
        factor = cols / cols[j : j + 1, :]
        state = state - jnp.where(row > j, factor, 0.0) * state[j : j + 1, :]
    out = []
    for k in range(2):
        diag = jnp.sum(jnp.where(lane == row + 32 * k, state, 0.0), axis=1, keepdims=True)
        out.append(state[:, 64 + 32 * k : 96 + 32 * k] * (1.0 / jnp.sqrt(diag)))
    return out


def kernel(
    scale,
    order_ref, tok_ref, cot_ref, gain_ref, w_ref, wo_ref, errq_ref, erro_ref, qq_ref, qo_ref,
    dtok_ref, gradq_ref, grado_ref, nerrq_ref, nerro_ref, bq_ref, bo_ref,
    W, WO, back, n, nt, xh, rstd, d, dn, qkvc,
    gbuf, xr, zs, zr, gobuf, xro, zso, zro, mq, mo,
    lr, gx, gz, tb, er1, t1, ex, t2, ey, ez, R,
    az_s, az_r, ax_s, ax_r, ay_s, ay_r, ac_s, ac_r,
    rx_s, rx_r, rz_s, rz_r, ro_s,
    l_s, l_r, gx_s, gx_r, gz_s, gz_r, e_s, e_r,
):
    r = lax.axis_index("rep")
    f = lax.axis_index("fsdp")
    y = r // 2
    c = r % 2
    z = f // 4
    x = f % 4

    def zp(dz):
        return (r, ((z + dz) % 8) * 4 + x)

    def xp(dx):
        return (r, z * 4 + (x + dx) % 4)

    def yp(dy):
        return (((y + dy) % 4) * 2 + c, f)

    cp = (y * 2 + 1 - c, f)

    def rp(k):
        return ((r + k) % 8, f)

    barrier = pltpu.get_barrier_semaphore()
    for k in range(1, 8):
        pl.semaphore_signal(barrier, inc=1, device_id=zp(k), device_id_type=MESH)
        pl.semaphore_signal(barrier, inc=1, device_id=rp(k), device_id_type=MESH)
    for k in range(1, 4):
        pl.semaphore_signal(barrier, inc=1, device_id=xp(k), device_id_type=MESH)

    def fr(w):
        front_window(w, order_ref, tok_ref, cot_ref, gain_ref, back, n, xh, rstd)

    source = (x // 2) == c

    @pl.when(source)
    def _():
        for k in range(3):
            W[y, z, x, :, 128 * k : 128 * k + 128] = w_ref[
                :, pl.ds(pl.multiple_of(512 * k + y * 128, 128), 128)
            ]

        @pl.when((z // 2) == y)
        def _():
            WO[z, x] = wo_ref[...]

    fr(0)
    pl.semaphore_wait(barrier, 17)

    @pl.when(source)
    def _():
        for k in range(1, 8):
            remote(W.at[y, z, x], W.at[y, z, x], az_s.at[0, k - 1], az_r.at[0, k - 1], zp(k)).start()

        @pl.when((z // 2) == y)
        def _():
            for k in range(1, 8):
                remote(WO.at[z, x], WO.at[z, x], az_s.at[1, k - 1], az_r.at[1, k - 1], zp(k)).start()

    fr(1)
    fr(2)

    @pl.when(source)
    def _():
        for k in range(1, 8):
            src = (z - k + 8) % 8
            remote(W.at[y, src, x], W.at[y, src, x], az_s.at[0, k - 1], az_r.at[0, k - 1], zp(k)).wait_recv()

            @pl.when((src // 2) == y)
            def _():
                remote(WO.at[src, x], WO.at[src, x], az_s.at[1, k - 1], az_r.at[1, k - 1], zp(k)).wait_recv()

        for k in range(1, 4):
            remote(W.at[y, :, x], W.at[y, :, x], ax_s.at[0, k - 1], ax_r.at[0, k - 1], xp(k)).start()
            o = WO.at[pl.ds(2 * y, 2), x]
            remote(o, o, ax_s.at[1, k - 1], ax_r.at[1, k - 1], xp(k)).start()

    fr(3)
    nt[...] = n[...].T

    for k in range(1, 4):
        src = (x - k + 4) % 4

        @pl.when((src // 2) == c)
        def _():
            remote(W.at[y, :, src], W.at[y, :, src], ax_s.at[0, k - 1], ax_r.at[0, k - 1], xp(k)).wait_recv()
            o = WO.at[pl.ds(2 * y, 2), src]
            remote(o, o, ax_s.at[1, k - 1], ax_r.at[1, k - 1], xp(k)).wait_recv()

    def dy_of(s):
        return s + (s // 2) * (1 - 2 * (s % 2))

    def hp_of(s):
        return (y - dy_of(s) + 4) % 4

    def half(hp, core):
        return W.at[hp, :, pl.ds(2 * core, 2)], WO.at[pl.ds(2 * hp, 2), pl.ds(2 * core, 2)]

    def core_copy(s, core):
        a, b = half(hp_of(s), core)
        return (
            remote(a, a, ac_s.at[0, s], ac_r.at[0, s], cp),
            remote(b, b, ac_s.at[1, s], ac_r.at[1, s], cp),
        )

    def y_copy(dy, hp):
        a, b = half(hp, c)
        return (
            remote(a, a, ay_s.at[0, dy - 1], ay_r.at[0, dy - 1], yp(dy)),
            remote(b, b, ay_s.at[1, dy - 1], ay_r.at[1, dy - 1], yp(dy)),
        )

    for cc in core_copy(0, c):
        cc.start()
    for dy in (1, 3, 2):
        for cc in y_copy(dy, y):
            cc.start()

    def x_send(s, k):
        to = (x + k) % 4
        return (
            remote(gbuf.at[s, :, to], xr.at[s, k - 1], rx_s.at[0, s, k - 1], rx_r.at[0, s, k - 1], xp(k)),
            remote(gobuf.at[s, :, to], xro.at[s, k - 1], rx_s.at[1, s, k - 1], rx_r.at[1, s, k - 1], xp(k)),
        )

    def z_send(s, k):
        return remote(
            zs.at[s, (z + k) % 8], zr.at[s, k - 1], rz_s.at[0, s, k - 1], rz_r.at[0, s, k - 1], zp(k)
        )

    def zo_send(s, j, k):
        return remote(zso.at[s, j], zro.at[k - 1], ro_s.at[s, j], rz_r.at[1, 0, k - 1], zp(k))

    def zo_each(s, act):
        for j in range(2):
            k = (2 * hp_of(s) + j - z + 8) % 8

            @pl.when(k > 0)
            def _():
                act(zo_send(s, j, k))

    def second(s):
        for k in range(1, 4):
            for cc in x_send(s, k):
                cc.wait_recv()
        total = gbuf[s, :, x].astype(f32)
        totalo = gobuf[s, :, x].astype(f32)
        for k in range(3):
            total = total + xr[s, k].astype(f32)
            totalo = totalo + xro[s, k].astype(f32)
        zs[s] = total.astype(bf16)
        zso[s] = totalo.astype(bf16)
        for k in range(1, 8):
            z_send(s, k).start()
        zo_each(s, lambda cc: cc.start())

    def step(s, carry):
        hp = hp_of(s)
        for cc in core_copy(s, 1 - c):
            cc.wait_recv()

        def mid():
            @pl.when(s < 3)
            def _():
                dy = dy_of(s + 1)
                for cc in y_copy(dy, hp_of(s + 1)):
                    cc.wait_recv()
                for cc in core_copy(s + 1, c):
                    cc.start()

        def g_store(v):
            gbuf[s] = v.reshape(8, 4, 16, 384)

        def go_store(v):
            gobuf[s] = v.reshape(2, 4, 16, 512)

        pair(
            n, nt, back, W[hp].reshape(512, 384), WO[pl.ds(2 * hp, 2)].reshape(128, 512),
            d, dn, qkvc, scale, s == 0, g_store, go_store, mid,
        )
        for k in range(1, 4):
            for cc in x_send(s, k):
                cc.start()

        @pl.when(s > 0)
        def _():
            second(s - 1)

        return carry

    lax.fori_loop(0, 4, step, 0)

    tail_norm(dn, xh, rstd, gain_ref, back, qkvc)
    second(3)
    tail_put(order_ref, qkvc, dtok_ref)

    def collect(s, carry):
        hp = hp_of(s)
        total = zs[s, z].astype(f32)
        for k in range(1, 8):
            z_send(s, k).wait_recv()
            total = total + zr[s, k - 1].astype(f32)
        for k in range(3):
            at = pl.ds(pl.multiple_of(512 * k + hp * 128, 128), 128)
            mq[:, at] = total[:, 128 * k : 128 * k + 128] + errq_ref[:, at]
        return carry

    lax.fori_loop(0, 4, collect, 0)
    for k in range(1, 8):
        zo_send(0, 0, k).wait_recv()
    so = dy_of((y - z // 2 + 4) % 4)
    total = zso[so, z % 2].astype(f32)
    for k in range(7):
        total = total + zro[k].astype(f32)
    mo[...] = total + erro_ref[...]

    mqv = mq[...]
    mov = mo[...]
    bqi = jnp.concatenate([qq_ref[...].astype(f32), jnp.zeros((96, 1536), f32)], 0).astype(bf16)
    boi = jnp.concatenate(
        [jnp.zeros((32, 512), f32), qo_ref[...].astype(f32), jnp.zeros((64, 512), f32)], 0
    ).astype(bf16)
    part = dnt(split3(mqv), bqi) + dnt(split3(mov), boi)
    lr[r] = ((part[0:16] + part[16:32]) + part[32:48]) * (1.0 / 127.0)
    for k in range(1, 8):
        remote(lr.at[r], lr.at[r], l_s.at[k - 1], l_r.at[k - 1], rp(k)).start()
    for k in range(1, 8):
        src = (r - k + 8) % 8
        remote(lr.at[src], lr.at[src], l_s.at[k - 1], l_r.at[k - 1], rp(k)).wait_recv()
    left = lr[0]
    for k in range(1, 8):
        left = left + lr[k]
    left = left * 0.125

    lt = left.T
    lane = lax.broadcasted_iota(jnp.int32, (32, 128), 1)
    full = hdot(lt, left)
    gx[x] = jnp.where(lane < 32, full[0:32], jnp.where(lane < 64, full[32:64], 0.0))
    for k in range(1, 4):
        remote(gx.at[x], gx.at[x], gx_s.at[k - 1], gx_r.at[k - 1], xp(k)).start()
    tq = hdot(lt[0:32], mqv)
    to = hdot(lt[32:64], mov)
    for k in range(12):
        tb[k] = tq[:, 128 * k : 128 * k + 128]
    for k in range(4):
        tb[12 + k] = to[:, 128 * k : 128 * k + 128]
    e1 = remote(tb.at[pl.ds(8 * (1 - c), 8)], er1, e_s.at[0, 0], e_r.at[0, 0], cp)
    e1.start()
    for k in range(1, 4):
        src = (x - k + 4) % 4
        remote(gx.at[src], gx.at[src], gx_s.at[k - 1], gx_r.at[k - 1], xp(k)).wait_recv()
    gz[z] = (gx[0] + gx[1]) + (gx[2] + gx[3])
    for k in range(1, 8):
        remote(gz.at[z], gz.at[z], gz_s.at[k - 1], gz_r.at[k - 1], zp(k)).start()
    e1.wait_recv()
    t1[...] = (tb[pl.ds(8 * c, 8)] + er1[...]).reshape(4, 2, 32, 128)
    e2 = [
        remote(t1.at[(x + k) % 4], ex.at[k - 1], e_s.at[1, k - 1], e_r.at[1, k - 1], xp(k))
        for k in range(1, 4)
    ]
    for cc in e2:
        cc.start()
    for cc in e2:
        cc.wait_recv()
    t2[...] = ((t1[x] + ex[0]) + (ex[1] + ex[2])).reshape(4, 16, 128)
    e3 = [
        remote(t2.at[(y + k) % 4], ey.at[k - 1], e_s.at[2, k - 1], e_r.at[2, k - 1], yp(k))
        for k in range(1, 4)
    ]
    for cc in e3:
        cc.start()
    for cc in e3:
        cc.wait_recv()
    ez[z] = (t2[y] + ey[0]) + (ey[1] + ey[2])
    for k in range(1, 8):
        remote(ez.at[z], ez.at[z], e_s.at[3, k - 1], e_r.at[3, k - 1], zp(k)).start()
    for k in range(1, 8):
        src = (z - k + 8) % 8
        remote(gz.at[src], gz.at[src], gz_s.at[k - 1], gz_r.at[k - 1], zp(k)).wait_recv()
    gram = gz[0]
    for k in range(1, 8):
        gram = gram + gz[k]
    iq, io = inverse_factors(gram)
    ortho_q = dnt_hi(left[:, 0:32], iq)
    ortho_o = dnt_hi(left[:, 32:64], io)
    for k in range(1, 8):
        src = (z - k + 8) % 8
        remote(ez.at[src], ez.at[src], e_s.at[3, k - 1], e_r.at[3, k - 1], zp(k)).wait_recv()
    t4 = ez[0]
    for k in range(1, 8):
        t4 = t4 + ez[k]
    R[c, x, y] = t4
    for k in range(1, 4):
        remote(R.at[c, x, y], R.at[c, x, y], e_s.at[4, k - 1], e_r.at[4, k - 1], yp(k)).start()
    for k in range(1, 4):
        src = (y - k + 4) % 4
        remote(R.at[c, x, src], R.at[c, x, src], e_s.at[4, k - 1], e_r.at[4, k - 1], yp(k)).wait_recv()
    for k in range(1, 4):
        remote(R.at[c, x], R.at[c, x], e_s.at[5, k - 1], e_r.at[5, k - 1], xp(k)).start()
    for k in range(1, 4):
        src = (x - k + 4) % 4
        remote(R.at[c, src], R.at[c, src], e_s.at[5, k - 1], e_r.at[5, k - 1], xp(k)).wait_recv()
    remote(R.at[c], R.at[c], e_s.at[6, 0], e_r.at[6, 0], cp).start()
    remote(R.at[1 - c], R.at[1 - c], e_s.at[6, 0], e_r.at[6, 0], cp).wait_recv()

    blocks = R[...].reshape(16, 32, 128)
    right_q = hdot(iq, jnp.concatenate([blocks[k] for k in range(12)], 1)) * 0.125
    right_o = hdot(io, jnp.concatenate([blocks[12 + k] for k in range(4)], 1)) * 0.125
    bq_ref[...] = right_q
    bo_ref[...] = right_o
    grad_q = hdot(ortho_q, right_q)
    grad_o = hdot(ortho_o, right_o)
    gradq_ref[...] = grad_q
    grado_ref[...] = grad_o
    nerrq_ref[...] = mqv - grad_q
    nerro_ref[...] = mov - grad_o

    @pl.when(source)
    def _():
        for k in range(1, 8):
            remote(W.at[y, z, x], W.at[y, z, x], az_s.at[0, k - 1], az_r.at[0, k - 1], zp(k)).wait_send()

        @pl.when((z // 2) == y)
        def _():
            for k in range(1, 8):
                remote(WO.at[z, x], WO.at[z, x], az_s.at[1, k - 1], az_r.at[1, k - 1], zp(k)).wait_send()

        for k in range(1, 4):
            remote(W.at[y, :, x], W.at[y, :, x], ax_s.at[0, k - 1], ax_r.at[0, k - 1], xp(k)).wait_send()
            o = WO.at[pl.ds(2 * y, 2), x]
            remote(o, o, ax_s.at[1, k - 1], ax_r.at[1, k - 1], xp(k)).wait_send()

    for dy in (1, 3, 2):
        for cc in y_copy(dy, y):
            cc.wait_send()

    def sent(s, carry):
        for cc in core_copy(s, c):
            cc.wait_send()
        for k in range(1, 4):
            for cc in x_send(s, k):
                cc.wait_send()
        for k in range(1, 8):
            z_send(s, k).wait_send()
        zo_each(s, lambda cc: cc.wait_send())
        return carry

    lax.fori_loop(0, 4, sent, 0)
    for k in range(1, 8):
        remote(lr.at[r], lr.at[r], l_s.at[k - 1], l_r.at[k - 1], rp(k)).wait_send()
        remote(gz.at[z], gz.at[z], gz_s.at[k - 1], gz_r.at[k - 1], zp(k)).wait_send()
        remote(ez.at[z], ez.at[z], e_s.at[3, k - 1], e_r.at[3, k - 1], zp(k)).wait_send()
    e1.wait_send()
    for k in range(1, 4):
        remote(gx.at[x], gx.at[x], gx_s.at[k - 1], gx_r.at[k - 1], xp(k)).wait_send()
        e2[k - 1].wait_send()
        e3[k - 1].wait_send()
        remote(R.at[c, x, y], R.at[c, x, y], e_s.at[4, k - 1], e_r.at[4, k - 1], yp(k)).wait_send()
        remote(R.at[c, x], R.at[c, x], e_s.at[5, k - 1], e_r.at[5, k - 1], xp(k)).wait_send()
    remote(R.at[c], R.at[c], e_s.at[6, 0], e_r.at[6, 0], cp).wait_send()


def per_device(tokens, cotangent, window_order, gain, w_qkv, w_out, err_qkv, err_out, q_qkv, q_out):
    scale = float(lax.axis_size("fsdp") * tokens.shape[0]) ** (-0.5)
    vmem = pl.BlockSpec(memory_space=pltpu.VMEM)
    V = pltpu.VMEM
    dma = pltpu.SemaphoreType.DMA
    outs = pl.pallas_call(
        functools.partial(kernel, scale),
        out_shape=(
            jax.ShapeDtypeStruct((576, 512), bf16),
            jax.ShapeDtypeStruct((16, 1536), f32),
            jax.ShapeDtypeStruct((16, 512), f32),
            jax.ShapeDtypeStruct((16, 1536), f32),
            jax.ShapeDtypeStruct((16, 512), f32),
            jax.ShapeDtypeStruct((32, 1536), f32),
            jax.ShapeDtypeStruct((32, 512), f32),
        ),
        in_specs=[vmem] * 10,
        out_specs=(vmem,) * 7,
        scratch_shapes=[
            V((4, 8, 4, 16, 384), bf16), V((8, 4, 16, 512), bf16),
            V((576, 512), bf16), V((576, 512), bf16), V((512, 576), bf16),
            V((576, 512), f32), V((576, 1), f32), V((576, 384), bf16), V((576, 512), f32), V((576, 512), bf16),
            V((4, 8, 4, 16, 384), bf16), V((4, 3, 8, 16, 384), bf16), V((4, 8, 16, 384), bf16), V((4, 7, 16, 384), bf16),
            V((4, 2, 4, 16, 512), bf16), V((4, 3, 2, 16, 512), bf16), V((4, 2, 16, 512), bf16), V((7, 16, 512), bf16),
            V((16, 1536), f32), V((16, 512), f32),
            V((8, 16, 128), f32), V((4, 32, 128), f32), V((8, 32, 128), f32),
            V((16, 32, 128), f32), V((8, 32, 128), f32), V((4, 2, 32, 128), f32), V((3, 2, 32, 128), f32),
            V((4, 16, 128), f32), V((3, 16, 128), f32), V((8, 16, 128), f32), V((2, 4, 4, 16, 128), f32),
            dma((2, 7)), dma((2, 7)), dma((2, 3)), dma((2, 3)), dma((2, 3)), dma((2, 3)), dma((2, 4)), dma((2, 4)),
            dma((2, 4, 3)), dma((2, 4, 3)), dma((1, 4, 7)), dma((2, 4, 7)), dma((4, 2)),
            dma((7,)), dma((7,)), dma((3,)), dma((3,)), dma((7,)), dma((7,)), dma((7, 7)), dma((7, 7)),
        ],
        compiler_params=pltpu.CompilerParams(
            collective_id=0, has_side_effects=True, vmem_limit_bytes=48 * 2**20
        ),
    )(
        window_order, tokens, cotangent, gain.reshape(1, 512), w_qkv, w_out,
        err_qkv.reshape(16, 1536), err_out.reshape(16, 512), q_qkv.T, q_out.T,
    )
    dt, gq, go, eq, eo, bq, bo = outs
    return dt, gq, go, eq[None], eo[None], bq.T, bo.T


def solution(mesh):
    return jax.shard_map(
        per_device,
        mesh=mesh,
        in_specs=(
            P(("rep", "fsdp"), None),
            P(("rep", "fsdp"), None),
            P(("rep", "fsdp"), None),
            P(),
            P("fsdp", None),
            P("fsdp", None),
            P("rep", "fsdp", None),
            P("rep", "fsdp", None),
            P(),
            P(),
        ),
        out_specs=(
            P(("rep", "fsdp"), None),
            P("fsdp", None),
            P("fsdp", None),
            P("rep", "fsdp", None),
            P("rep", "fsdp", None),
            P(),
            P(),
        ),
        check_vma=False,
    )
```

time: 996 us -> 112 us (0.11)
  waiting for transfers between devices: 695 us -> 0 us
  blocking collectives: 182 us -> 0 us
  Pallas kernels: 0 us -> 98.9 us
  other arithmetic: 34.6 us -> 0 us
  matrix products: 31.4 us -> 0 us
  local copies, waits for them, and re-layouts: 36.5 us -> 12.4 us
  between operations: 14.4 us -> 0.67 us
    reduce_scatter x2 -> x0, waiting for transfers between devices: 400 us -> none  [the longest x1 218 us: per_device(): lax.psum_scatter((lax.dot_general(columns, d_qkv, (((0,), (0,)), ((), ())...]
    psum x1 -> x0, waiting for transfers between devices: 267 us -> none  [per_device(): right_qkv, right_out = lax.psum((right_qkv, right_out), ('rep', 'fsdp'))]
    psum x2 -> x0, blocking collectives: 139 us -> none  [the longest x1 113 us: per_device(): lax.psum((jnp.dot(left_qkv.T, left_qkv, precision=highest), jnp.dot(left_...]
    pallas_call x0 -> x1, Pallas kernels: none -> 98.9 us  [per_device(): pl.pallas_call(functools.partial(kernel, scale), out_shape=(jax.ShapeDtyp...]
    all_gather x1 -> x0, blocking collectives: 43.1 us -> none  [per_device(): lax.all_gather(w_out, 'fsdp', axis=0, tiled=True)]
    dot_general x19 -> x0, matrix products: 31 us -> none  [the longest x3 8.73 us: attend(): scores = jnp.einsum('nqhd,nkhd->nhqk', query, key_part) * size ** (-0.5)]
    all_gather x1 -> x0, waiting for transfers between devices: 26.7 us -> none  [per_device(): lax.all_gather(w_qkv, 'fsdp', axis=0, tiled=True)]
    reshape x4 -> x0, local copies, waits for them, and re-layouts: 13.7 us -> none  [the longest x1 5.38 us: per_device(): a.reshape(-1, WT, 3 * width)]
  transfers between devices with their start and end apart: 4 -> 0, of which waited for: 4 -> 0; matrix products, arithmetic and copies ran while one was open for 5% -> 0% of each run, Pallas kernels for 0% -> 0%
where the time goes in v1:
time: 112 us
  Pallas kernels  98.9 us (88%)
  local copies, waits for them, and re-layouts  12.4 us (11%)
    pallas_call x1, Pallas kernels, per_device(): pl.pallas_call(functools.partial(kernel, scale), out_shape=(jax.ShapeDtyp...  98.9 us
    unnamed x27, local copies, waits for them, and re-layouts  12.4 us

profile of v1, /device:TPU:1, one launch (start us, length us, event | category | flops | bytes accessed | tf_op | source)
XLA Modules:
  0.0 112.0 jit_solution(14911242482046086641)
XLA Ops:
  0.6 0.0 copy-start.8
  0.6 0.0 copy-start.9
  0.7 0.7 copy-done.8
  1.3 0.0 copy-done.9
  1.3 0.0 copy-start
  1.3 1.1 copy-done
  2.4 0.0 copy-start.1
  2.4 1.1 copy-done.1
  3.5 0.0 copy-start.2
  3.5 0.9 copy-done.2
  4.4 0.0 copy-start.3
  4.4 0.9 copy-done.3
  5.3 0.0 copy-start.4
  5.3 0.8 copy-done.4
  6.1 0.0 copy-start.5
  6.1 0.8 copy-done.5
  6.9 0.0 copy-start.6
  6.9 0.8 copy-done.6
  7.7 0.0 copy-start.7
  7.7 0.7 copy-done.7
  8.4 98.9 %shard_map.153 = (bf16[576,512]{1,0:T(8,128)(2,1)S(1)}, f32[16,1536]{1,0:T(8,128)S(1)}, f32[16,512]{1,0:T(8,128)S(1)}, f32[16,1536]{1,0:T(8,128)S(1)}, f32[16,51...) custom-call(s32[1,576]{1,0:T(1,128)S(1)} %copy-done.8, bf16[576,512]{1,0:T(8,128)(2,1)S(1)} %copy-done, ...), custom_call_target="tpu_custom_call" | custom-call | tf_op jit(solution)/shard_map/pallas_call | solution.py:506
  107.4 0.8 copy.24
  108.2 0.6 copy.25
  108.8 0.6 copy.26
  109.4 0.6 copy.27
  110.1 0.6 copy.28
  110.7 0.7 copy.29
  111.4 0.6 copy.30
Async XLA Ops:
  0.6 0.7 copy-start.8
  0.6 0.7 copy-start.9
  1.3 1.1 copy-start
  2.4 1.1 copy-start.1
  3.5 0.9 copy-start.2
  4.4 0.9 copy-start.3
  5.3 0.8 copy-start.4
  6.1 0.8 copy-start.5
  6.9 0.8 copy-start.6
  7.7 0.7 copy-start.7

commit v2 on v1

v2 whole, which is shorter than its diff:
```python
import functools

import jax
import jax.numpy as jnp
from jax import lax
from jax.experimental import pallas as pl
from jax.experimental.pallas import tpu as pltpu
from jax.sharding import PartitionSpec as P

f32 = jnp.float32
bf16 = jnp.bfloat16
MESH = pl.DeviceIdType.MESH
def dot(a,b): return jnp.dot(a,b,preferred_element_type=f32)
def dnt(a,b): return lax.dot_general(a,b,(((1,),(1,)),((),())),preferred_element_type=f32)
WT=144; NW=4
LOG2E=1.4426950408889634
def front_window(w,order_ref,tok_ref,cot_ref,gain_ref,back_ref,n_ref,xh_ref,rstd_ref):
        row=order_ref[...]
        T=row.shape[1]
        gain=gain_ref[...]
        sl=pl.ds(w*WT,WT)
        si=lax.broadcasted_iota(jnp.int32,(WT,T),0)+w*WT
        li=lax.broadcasted_iota(jnp.int32,(WT,T),1)
        col=jnp.sum(jnp.where(si==li,row,0).astype(f32),axis=1,keepdims=True).astype(jnp.int32)
        oh=jnp.where(col==li,1.0,0.0).astype(bf16)
        x=dot(oh,tok_ref[...])
        back_ref[sl,:]=dot(oh,cot_ref[...]).astype(bf16)
        ce=x-jnp.mean(x,-1,keepdims=True)
        rs=lax.rsqrt(jnp.mean(ce*ce,-1,keepdims=True)+1e-5)
        xh=ce*rs
        xh_ref[sl,:]=xh
        rstd_ref[sl,:]=rs
        n=(xh*gain).astype(bf16)
        n_ref[sl,:]=n
def pair(n_ref,nt_ref,back_ref,W,WO,d_ref,dn_ref,qkvc_ref,scale,first,g_store,go_store,mid=None):
    qkvc_ref[:,:384]=dot(n_ref[...],W).astype(bf16)
    qkvc_ref[:,384:]=dnt(back_ref[...],WO).astype(bf16)
    if mid is not None: mid()
    lane=lax.broadcasted_iota(jnp.int32,(WT,128),1)
    go=jnp.zeros((128,512),f32)
    for w in range(NW):
        sl=pl.ds(w*WT,WT)
        q=qkvc_ref[sl,0:128]; k=qkvc_ref[sl,128:256]; v=qkvc_ref[sl,256:384]; c=qkvc_ref[sl,384:512]
        qt=q.T; kt=k.T; vt=v.T; ct=c.T
        cts=[];dqs=[]
        dv=jnp.zeros((WT,128),f32); dk=jnp.zeros((WT,128),f32)
        for h in range(2):
            m=(lane<64) if h==0 else (lane>=64)
            z=jnp.zeros((),bf16)
            s=dot(jnp.where(m,k,z),qt)
            mx=jnp.max(s,axis=0,keepdims=True)
            e=jnp.exp2((s-mx)*(0.125*LOG2E))
            wt=e*(1.0/jnp.sum(e,axis=0,keepdims=True))
            p=wt.astype(bf16)
            cts.append(dot(vt[64*h:64*h+64],p))
            dp=dot(jnp.where(m,v,z),ct).astype(bf16).astype(f32)
            t=wt*dp
            ds=(t-wt*jnp.sum(t,axis=0,keepdims=True)).astype(bf16)
            dv=dv+dot(p,jnp.where(m,c,z))
            dk=dk+dot(ds,jnp.where(m,q,z))
            dqs.append(dot(kt[64*h:64*h+64],ds))
        ctx=jnp.concatenate(cts,0).astype(bf16)
        go=go+dot(ctx,back_ref[sl,:])
        dq=(jnp.concatenate(dqs,0)*0.125).astype(bf16).T
        d_ref[sl,0:128]=dq
        d_ref[sl,128:256]=(dk*0.125).astype(bf16)
        d_ref[sl,256:384]=dv.astype(bf16)
    go_store((go*scale).astype(bf16))
    g_store((dot(nt_ref[...],d_ref[...])*scale).astype(bf16))
    dn=dnt(d_ref[...],W)
    dn_ref[...]=jnp.where(first,0.0,dn_ref[...])+dn
def tail_norm(dn_ref,xh_ref,rstd_ref,gain_ref,back_ref,dwin_ref):
    gain=gain_ref[...]
    for w in range(NW):
        sl=pl.ds(w*WT,WT)
        dx=dn_ref[sl,:].astype(bf16).astype(f32)*gain
        xh=xh_ref[sl,:]
        d=rstd_ref[sl,:]*(dx-jnp.mean(dx,-1,keepdims=True)-xh*jnp.mean(dx*xh,-1,keepdims=True))
        dwin_ref[sl,:]=(back_ref[sl,:].astype(f32)+d).astype(bf16)

def tail_put(order_ref,dwin_ref,out_ref):
    row=order_ref[...]
    T=row.shape[1]
    for w in range(NW):
        sl=pl.ds(w*WT,WT)
        si=lax.broadcasted_iota(jnp.int32,(WT,T),0)+w*WT
        oh=jnp.where(si==row,1.0,0.0).astype(bf16)
        out_ref[sl,:]=dot(oh,dwin_ref[...]).astype(bf16)


def remote(src, dst, ss, rs, dev):
    return pltpu.make_async_remote_copy(
        src_ref=src, dst_ref=dst, send_sem=ss, recv_sem=rs, device_id=dev, device_id_type=MESH
    )


def split3(v):
    a = v.astype(bf16)
    r = v - a.astype(f32)
    b = r.astype(bf16)
    c = (r - b.astype(f32)).astype(bf16)
    return jnp.concatenate([a, b, c], 0)


def pieces(v):
    a = v.astype(bf16)
    r = v - a.astype(f32)
    b = r.astype(bf16)
    return a, b, (r - b.astype(f32)).astype(bf16)


def hdot(a, b):
    rows = a.shape[0]
    b1, b2, b3 = pieces(b)
    a3 = split3(a)
    u = dot(a3, b1)
    v = dot(a3[: 2 * rows], b2)
    w = dot(a3[:rows], b3)
    return u[:rows] + ((u[rows : 2 * rows] + v[:rows]) + (u[2 * rows :] + (v[rows:] + w)))


def inverse_factors(gram):
    lane = lax.broadcasted_iota(jnp.int32, (32, 128), 1)
    row = lax.broadcasted_iota(jnp.int32, (32, 128), 0)
    first = (lane % 64) < 32
    state = jnp.where(lane < 64, gram, jnp.where((lane % 32) == row, 1.0, 0.0))
    for j in range(31):
        cols = jnp.where(first, state[:, j : j + 1], state[:, 32 + j : 33 + j])
        factor = cols / cols[j : j + 1, :]
        state = state - jnp.where(row > j, factor, 0.0) * state[j : j + 1, :]
    out = []
    for k in range(2):
        diag = jnp.sum(jnp.where(lane == row + 32 * k, state, 0.0), axis=1, keepdims=True)
        out.append(state[:, 64 + 32 * k : 96 + 32 * k] * (1.0 / jnp.sqrt(diag)))
    return out


def kernel(
    scale,
    order_in, tok_in, cot_in, gain_in, w_in, wo_in, errq_in, erro_in, qq_in, qo_in,
    dtok_ref, R, left_ref, inv_ref, mq, mo,
    order_ref, tok_ref, cot_ref, gain_ref, w_ref, wo_ref, errq_ref, erro_ref, qq_ref, qo_ref, in_sem,
    W, WO, back, n, nt, xh, rstd, d, dn, qkvc,
    gbuf, xr, xm, zs, zr, gobuf, xro, xmo, zso, zro,
    lr, mb, mr, t1, ex, ez,
    az_s, az_r, ax_s, ax_r, ay_s, ay_r, ac_s, ac_r,
    rx_s, rx_r, rz_s, rz_r, ro_s,
    l_s, l_r, e_s, e_r,
):
    r = lax.axis_index("rep")
    f = lax.axis_index("fsdp")
    y = r // 2
    c = r % 2
    z = f // 4
    x = f % 4

    def zp(dz):
        return (r, ((z + dz) % 8) * 4 + x)

    def xp(dx):
        return (r, z * 4 + (x + dx) % 4)

    def yp(dy):
        return (((y + dy) % 4) * 2 + c, f)

    cp = (y * 2 + 1 - c, f)

    def rp(k):
        return ((r + k) % 8, f)

    loads = [
        pltpu.make_async_copy(a, b, in_sem.at[k])
        for k, (a, b) in enumerate(
            (
                (w_in, w_ref), (wo_in, wo_ref), (order_in, order_ref), (gain_in, gain_ref), (tok_in, tok_ref),
                (cot_in, cot_ref), (errq_in, errq_ref), (erro_in, erro_ref), (qq_in, qq_ref), (qo_in, qo_ref),
            )
        )
    ]
    for cc in loads:
        cc.start()
    barrier = pltpu.get_barrier_semaphore()
    for k in range(1, 8):
        pl.semaphore_signal(barrier, inc=1, device_id=zp(k), device_id_type=MESH)
        pl.semaphore_signal(barrier, inc=1, device_id=rp(k), device_id_type=MESH)
    for k in range(1, 4):
        pl.semaphore_signal(barrier, inc=1, device_id=xp(k), device_id_type=MESH)

    def fr(w):
        front_window(w, order_ref, tok_ref, cot_ref, gain_ref, back, n, xh, rstd)

    source = (x // 2) == c
    for cc in loads[:6]:
        cc.wait()

    own = y % 2

    @pl.when(source)
    def _():
        for i in range(2):
            for k in range(3):
                W[2 * own + i, z, x, :, 128 * k : 128 * k + 128] = w_ref[
                    :, pl.ds(pl.multiple_of(512 * k + (2 * own + i) * 128, 128), 128)
                ]

        @pl.when((z // 4) == own)
        def _():
            WO[z, x] = wo_ref[...]

    fr(0)
    pl.semaphore_wait(barrier, 17)

    def w_z(i, k, at):
        a = W.at[2 * own + i, at, x]
        return remote(a, a, az_s.at[i, k - 1], az_r.at[i, k - 1], zp(k))

    def wo_z(k, at):
        a = WO.at[at, x]
        return remote(a, a, az_s.at[2, k - 1], az_r.at[2, k - 1], zp(k))

    def w_x(i, k, at):
        a = W.at[2 * own + i, :, at]
        b = WO.at[pl.ds(2 * (2 * own + i), 2), at]
        return (
            remote(a, a, ax_s.at[0, i, k - 1], ax_r.at[0, i, k - 1], xp(k)),
            remote(b, b, ax_s.at[1, i, k - 1], ax_r.at[1, i, k - 1], xp(k)),
        )

    def wait_x(i):
        for k in range(1, 4):
            src = (x - k + 4) % 4

            @pl.when((src // 2) == c)
            def _():
                for cc in w_x(i, k, src):
                    cc.wait_recv()

    @pl.when(source)
    def _():
        for i in range(2):
            for k in range(1, 8):
                w_z(i, k, z).start()
            if i == 0:

                @pl.when((z // 4) == own)
                def _():
                    for k in range(1, 8):
                        wo_z(k, z).start()

    fr(1)
    fr(2)

    @pl.when(source)
    def _():
        for i in range(2):
            for k in range(1, 8):
                src = (z - k + 8) % 8
                w_z(i, k, src).wait_recv()

                @pl.when((src // 2) == 2 * own + i)
                def _():
                    wo_z(k, src).wait_recv()

            for k in range(1, 4):
                for cc in w_x(i, k, x):
                    cc.start()

    fr(3)
    nt[...] = n[...].T

    def hp_of(s):
        return (2 * own + s) % 4

    def half(hp, core):
        return W.at[hp, :, pl.ds(2 * core, 2)], WO.at[pl.ds(2 * hp, 2), pl.ds(2 * core, 2)]

    def core_copy(s, core):
        a, b = half(hp_of(s), core)
        return (
            remote(a, a, ac_s.at[0, s], ac_r.at[0, s], cp),
            remote(b, b, ac_s.at[1, s], ac_r.at[1, s], cp),
        )

    def y_copy(i, hp):
        a, b = half(hp, c)
        to = yp((1 + 2 * own + 2 * i) % 4)
        return (
            remote(a, a, ay_s.at[0, i], ay_r.at[0, i], to),
            remote(b, b, ay_s.at[1, i], ay_r.at[1, i], to),
        )

    def spread(i):
        wait_x(i)
        for cc in y_copy(i, 2 * own + i):
            cc.start()
        for cc in core_copy(i, c):
            cc.start()

    spread(0)

    def x_copy(kind, s, way):
        to = xp(1 + 2 * way)
        h = 1 - way if kind == 1 else way
        if kind == 2:
            a, b = xm.at[s, way], xmo.at[s, pl.ds(way, 1)]
        else:
            at = (x + 2) % 4 if kind == 0 else (x + 1 + 2 * way) % 4
            a, b = gbuf.at[s, pl.ds(4 * h, 4), at], gobuf.at[s, pl.ds(h, 1), at]
        return (
            remote(a, xr.at[kind, s, way], rx_s.at[0, kind, s, way], rx_r.at[0, kind, s, way], to),
            remote(b, xro.at[kind, s, pl.ds(way, 1)], rx_s.at[1, kind, s, way], rx_r.at[1, kind, s, way], to),
        )

    def merge(s):
        for way in range(2):
            for cc in x_copy(0, s, way):
                cc.wait_recv()
            at = (x + 1 + 2 * way) % 4
            xm[s, way] = (gbuf[s, 4 * way : 4 * way + 4, at].astype(f32) + xr[0, s, way].astype(f32)).astype(bf16)
            xmo[s, way] = (gobuf[s, way, at].astype(f32) + xro[0, s, way].astype(f32)).astype(bf16)
            for cc in x_copy(2, s, way):
                cc.start()

    def z_send(s, k):
        return remote(
            zs.at[s, (z + k) % 8], zr.at[s, k - 1], rz_s.at[0, s, k - 1], rz_r.at[0, s, k - 1], zp(k)
        )

    def zo_send(s, j, k):
        return remote(zso.at[s, j], zro.at[k - 1], ro_s.at[s, j], rz_r.at[1, 0, k - 1], zp(k))

    def zo_each(s, act):
        for j in range(2):
            k = (2 * hp_of(s) + j - z + 8) % 8

            @pl.when(k > 0)
            def _():
                act(zo_send(s, j, k))

    def second(s):
        for kind in (1, 2):
            for way in range(2):
                for cc in x_copy(kind, s, way):
                    cc.wait_recv()
        for h in range(2):
            rows = slice(4 * h, 4 * h + 4)
            total = gbuf[s, rows, x].astype(f32) + (xr[1, s, 1 - h].astype(f32) + xr[2, s, h].astype(f32))
            zs[s, rows] = total.astype(bf16)
            total = gobuf[s, h, x].astype(f32) + (xro[1, s, 1 - h].astype(f32) + xro[2, s, h].astype(f32))
            zso[s, h] = total.astype(bf16)
        for k in range(1, 8):
            z_send(s, k).start()
        zo_each(s, lambda cc: cc.start())

    def step(s, carry):
        hp = hp_of(s)
        for cc in core_copy(s, 1 - c):
            cc.wait_recv()

        def mid():
            @pl.when(s == 0)
            def _():
                spread(1)

            @pl.when((s == 1) | (s == 2))
            def _():
                for cc in y_copy(s - 1, hp_of(s + 1)):
                    cc.wait_recv()
                for cc in core_copy(s + 1, c):
                    cc.start()

        def g_store(v):
            gbuf[s] = v.reshape(8, 4, 16, 384)

        def go_store(v):
            gobuf[s] = v.reshape(2, 4, 16, 512)

        pair(
            n, nt, back, W[hp].reshape(512, 384), WO[pl.ds(2 * hp, 2)].reshape(128, 512),
            d, dn, qkvc, scale, s == 0, g_store, go_store, mid,
        )
        for kind in (0, 1):
            for way in range(2):
                for cc in x_copy(kind, s, way):
                    cc.start()

        @pl.when(s > 0)
        def _():
            merge(s - 1)

        @pl.when(s > 1)
        def _():
            second(s - 2)

        return carry

    lax.fori_loop(0, 4, step, 0)

    tail_norm(dn, xh, rstd, gain_ref, back, qkvc)
    merge(3)
    second(2)
    tail_put(order_ref, qkvc, dtok_ref)
    second(3)

    for cc in loads[6:]:
        cc.wait()

    def collect(s, carry):
        hp = hp_of(s)
        total = zs[s, z].astype(f32)
        for k in range(1, 8):
            z_send(s, k).wait_recv()
            total = total + zr[s, k - 1].astype(f32)
        for k in range(3):
            at = pl.ds(pl.multiple_of(512 * k + hp * 128, 128), 128)
            mq[:, at] = total[:, 128 * k : 128 * k + 128] + errq_ref[:, at]
        return carry

    lax.fori_loop(0, 4, collect, 0)
    for k in range(1, 8):
        zo_send(0, 0, k).wait_recv()
    so = (z // 2 - 2 * own + 4) % 4
    total = zso[so, z % 2].astype(f32)
    for k in range(7):
        total = total + zro[k].astype(f32)
    mo[...] = total + erro_ref[...]

    mqv = mq[...]
    mov = mo[...]
    for k in range(12):
        mb[k // 2, k % 2] = mqv[:, 128 * k : 128 * k + 128]
    for k in range(4):
        mb[6 + k // 2, k % 2] = mov[:, 128 * k : 128 * k + 128]

    def m_copy(k):
        return remote(mb.at[(r + k) % 8], mr.at[k - 1], l_s.at[1, k - 1], l_r.at[1, k - 1], rp(k))

    def l_copy(k, at):
        return remote(lr.at[at], lr.at[at], l_s.at[0, k - 1], l_r.at[0, k - 1], rp(k))

    for k in range(1, 8):
        m_copy(k).start()
    bqi = jnp.concatenate([qq_ref[...].astype(f32), jnp.zeros((96, 1536), f32)], 0).astype(bf16)
    boi = jnp.concatenate(
        [jnp.zeros((32, 512), f32), qo_ref[...].astype(f32), jnp.zeros((64, 512), f32)], 0
    ).astype(bf16)
    part = dnt(split3(mqv), bqi) + dnt(split3(mov), boi)
    lr[r] = ((part[0:16] + part[16:32]) + part[32:48]) * (1.0 / 127.0)
    for k in range(1, 8):
        l_copy(k, r).start()
    for k in range(1, 8):
        m_copy(k).wait_recv()
    total = mb[r]
    for k in range(7):
        total = total + mr[k]
    for k in range(1, 8):
        l_copy(k, (r - k + 8) % 8).wait_recv()
    left = lr[0]
    for k in range(1, 8):
        left = left + lr[k]
    left = left * 0.125
    left_ref[...] = left

    lt = left.T
    lane = lax.broadcasted_iota(jnp.int32, (32, 128), 1)
    full = hdot(lt, left)
    gram = jnp.where(lane < 32, full[0:32], jnp.where(lane < 64, full[32:64], 0.0))
    mine = jnp.where(r < 6, lt[0:32], lt[32:64])
    for j in range(2):
        t = hdot(mine, total[j])
        t1[2 * j, 0:16] = t[0:16]
        t1[2 * j + 1, 0:16] = t[16:32]
    for k in range(4):
        t1[k, 16:48] = gram
    ex[x] = t1[x]

    def e_x(k, to, at):
        return remote(t1.at[to], ex.at[at], e_s.at[0, k - 1], e_r.at[0, k - 1], xp(k))

    def e_z(k, at):
        return remote(ez.at[at], ez.at[at], e_s.at[1, k - 1], e_r.at[1, k - 1], zp(k))

    def a_x(k, at):
        return remote(R.at[r, at], R.at[r, at], e_s.at[2, k - 1], e_r.at[2, k - 1], xp(k))

    def a_r(k, at):
        return remote(R.at[at], R.at[at], e_s.at[3, k - 1], e_r.at[3, k - 1], rp(k))

    for k in range(1, 4):
        e_x(k, (x + k) % 4, x).start()
    for k in range(1, 4):
        e_x(k, x, (x - k + 4) % 4).wait_recv()
    ez[z] = (ex[0] + ex[1]) + (ex[2] + ex[3])
    for k in range(1, 8):
        e_z(k, z).start()
    for k in range(1, 8):
        e_z(k, (z - k + 8) % 8).wait_recv()
    total = ez[0]
    for k in range(1, 8):
        total = total + ez[k]
    R[r, x] = total[0:16]
    for k in range(1, 4):
        a_x(k, x).start()
    iq, io = inverse_factors(total[16:48])
    inv_ref[0] = iq
    inv_ref[1] = io
    for k in range(1, 4):
        a_x(k, (x - k + 4) % 4).wait_recv()
    for k in range(1, 8):
        a_r(k, r).start()
    for k in range(1, 8):
        a_r(k, (r - k + 8) % 8).wait_recv()

    @pl.when(source)
    def _():
        for i in range(2):
            for k in range(1, 8):
                w_z(i, k, z).wait_send()
            for k in range(1, 4):
                for cc in w_x(i, k, x):
                    cc.wait_send()

        @pl.when((z // 4) == own)
        def _():
            for k in range(1, 8):
                wo_z(k, z).wait_send()

    for i in range(2):
        for cc in y_copy(i, 2 * own + i):
            cc.wait_send()

    def sent(s, carry):
        for cc in core_copy(s, c):
            cc.wait_send()
        for kind in range(3):
            for way in range(2):
                for cc in x_copy(kind, s, way):
                    cc.wait_send()
        for k in range(1, 8):
            z_send(s, k).wait_send()
        zo_each(s, lambda cc: cc.wait_send())
        return carry

    lax.fori_loop(0, 4, sent, 0)
    for k in range(1, 8):
        m_copy(k).wait_send()
        l_copy(k, r).wait_send()
        e_z(k, z).wait_send()
        a_r(k, r).wait_send()
    for k in range(1, 4):
        e_x(k, (x + k) % 4, x).wait_send()
        a_x(k, x).wait_send()


def finish(
    dtok_in, R, left_ref, inv_ref, mq_ref, mo_ref,
    dtok_out, gradq_out, grado_out, nerrq_out, nerro_out, bq_out, bo_out,
    gradq, grado, nerrq, nerro, bq, bo, sem,
):
    def out(k, a, b):
        cc = pltpu.make_async_copy(a, b, sem.at[k])
        cc.start()
        return cc

    outs = [out(0, dtok_in, dtok_out)]
    left = left_ref[...]
    iq = inv_ref[0]
    io = inv_ref[1]
    ortho_q = hdot(left[:, 0:32], iq.T)
    ortho_o = hdot(left[:, 32:64], io.T)
    blocks = R[...].reshape(16, 32, 128)
    bq[...] = hdot(iq, jnp.concatenate([blocks[k] for k in range(12)], 1)) * 0.125
    outs.append(out(1, bq, bq_out))
    bo[...] = hdot(io, jnp.concatenate([blocks[12 + k] for k in range(4)], 1)) * 0.125
    outs.append(out(2, bo, bo_out))
    grad = hdot(ortho_q, bq[...])
    gradq[...] = grad
    nerrq[...] = mq_ref[...] - grad
    outs.append(out(3, gradq, gradq_out))
    outs.append(out(4, nerrq, nerrq_out))
    grad = hdot(ortho_o, bo[...])
    grado[...] = grad
    nerro[...] = mo_ref[...] - grad
    outs.append(out(5, grado, grado_out))
    outs.append(out(6, nerro, nerro_out))
    for cc in outs:
        cc.wait()


def per_device(tokens, cotangent, window_order, gain, w_qkv, w_out, err_qkv, err_out, q_qkv, q_out):
    scale = float(lax.axis_size("fsdp") * tokens.shape[0]) ** (-0.5)
    vmem = pl.BlockSpec(memory_space=pltpu.VMEM)
    V = pltpu.VMEM
    dma = pltpu.SemaphoreType.DMA
    hbm = pl.BlockSpec(memory_space=pl.ANY)

    def shape(dims, kind=f32):
        return jax.ShapeDtypeStruct(dims, kind)

    mid = pl.pallas_call(
        functools.partial(kernel, scale),
        out_shape=(
            shape((576, 512), bf16), shape((8, 4, 16, 128)), shape((16, 128)), shape((2, 32, 32)),
            shape((16, 1536)), shape((16, 512)),
        ),
        in_specs=[hbm] * 10,
        out_specs=(vmem,) * 6,
        scratch_shapes=[
            V((1, 576), jnp.int32), V((576, 512), bf16), V((576, 512), bf16), V((1, 512), f32),
            V((16, 1536), bf16), V((16, 512), bf16), V((16, 1536), f32), V((16, 512), f32),
            V((32, 1536), jnp.int32), V((32, 512), jnp.int32), dma((10,)),
            V((4, 8, 4, 16, 384), bf16), V((8, 4, 16, 512), bf16),
            V((576, 512), bf16), V((576, 512), bf16), V((512, 576), bf16),
            V((576, 512), f32), V((576, 1), f32), V((576, 384), bf16), V((576, 512), f32), V((576, 512), bf16),
            V((4, 8, 4, 16, 384), bf16), V((3, 4, 2, 4, 16, 384), bf16), V((4, 2, 4, 16, 384), bf16), V((4, 8, 16, 384), bf16), V((4, 7, 16, 384), bf16),
            V((4, 2, 4, 16, 512), bf16), V((3, 4, 2, 16, 512), bf16), V((4, 2, 16, 512), bf16), V((4, 2, 16, 512), bf16), V((7, 16, 512), bf16),
            V((8, 16, 128), f32), V((8, 2, 16, 128), f32), V((7, 2, 16, 128), f32),
            V((4, 48, 128), f32), V((4, 48, 128), f32), V((8, 48, 128), f32),
            dma((3, 7)), dma((3, 7)), dma((2, 2, 3)), dma((2, 2, 3)), dma((2, 2)), dma((2, 2)), dma((2, 4)), dma((2, 4)),
            dma((2, 3, 4, 2)), dma((2, 3, 4, 2)), dma((1, 4, 7)), dma((2, 4, 7)), dma((4, 2)),
            dma((2, 7)), dma((2, 7)), dma((4, 7)), dma((4, 7)),
        ],
        compiler_params=pltpu.CompilerParams(
            collective_id=0, has_side_effects=True, vmem_limit_bytes=56 * 2**20
        ),
    )(
        window_order, tokens, cotangent, gain.reshape(1, 512), w_qkv, w_out,
        err_qkv.reshape(16, 1536), err_out.reshape(16, 512), q_qkv.T, q_out.T,
    )
    dt, gq, go, eq, eo, bq, bo = pl.pallas_call(
        finish,
        out_shape=(
            shape((576, 512), bf16), shape((16, 1536)), shape((16, 512)), shape((16, 1536)), shape((16, 512)),
            shape((32, 1536)), shape((32, 512)),
        ),
        in_specs=[vmem] * 6,
        out_specs=(hbm,) * 7,
        scratch_shapes=[
            V((16, 1536), f32), V((16, 512), f32), V((16, 1536), f32), V((16, 512), f32),
            V((32, 1536), f32), V((32, 512), f32), dma((7,)),
        ],
    )(*mid)
    return dt, gq, go, eq[None], eo[None], bq.T, bo.T


def solution(mesh):
    return jax.shard_map(
        per_device,
        mesh=mesh,
        in_specs=(
            P(("rep", "fsdp"), None),
            P(("rep", "fsdp"), None),
            P(("rep", "fsdp"), None),
            P(),
            P("fsdp", None),
            P("fsdp", None),
            P("rep", "fsdp", None),
            P("rep", "fsdp", None),
            P(),
            P(),
        ),
        out_specs=(
            P(("rep", "fsdp"), None),
            P("fsdp", None),
            P("fsdp", None),
            P("rep", "fsdp", None),
            P("rep", "fsdp", None),
            P(),
            P(),
        ),
        check_vma=False,
    )
```

time: 112 us -> 89.1 us (0.80)
  local copies, waits for them, and re-layouts: 12.4 us -> 0 us
  Pallas kernels: 98.9 us -> 88.3 us
    unnamed x27 -> x0, local copies, waits for them, and re-layouts: 12.4 us -> none
    pallas_call x1 -> x2, Pallas kernels: 98.9 us -> 88.3 us  [the longest x1 85.7 us: per_device(): pl.pallas_call(functools.partial(kernel, scale), out_shape=(shape((576, 5...]
where the time goes in v2:
time: 89.1 us; the launch traced here: 88.9 us
  Pallas kernels  88.3 us (99%)
    pallas_call x1, Pallas kernels, per_device(): pl.pallas_call(functools.partial(kernel, scale), out_shape=(shape((576, 5...  85.7 us
    pallas_call x1, Pallas kernels, per_device(): pl.pallas_call(finish, out_shape=(shape((576, 512), bf16), shape((16, 153...  2.56 us

profile of v2, /device:TPU:1, one launch (start us, length us, event | category | flops | bytes accessed | tf_op | source)
XLA Modules:
  0.0 88.9 jit_solution(14374661264762090549)
XLA Ops:
  0.6 85.7 %shard_map.153 = (bf16[576,512]{1,0:T(8,128)(2,1)}, f32[8,4,16,128]{3,2,1,0:T(8,128)}, f32[16,128]{1,0:T(8,128)}, f32[2,32,32]{2,1,0:T(8,128)}, f32[16,1536]{1,0:T(8,128)}, /*index=5*/f32[16,512]{1,0:T(8,128)}) custom-call(s32[1,576]{1,0:T(1,128)} %order_in.1, bf16[576,512]{1,0:T(8,128)(2,1)} %tok_in.1, bf16[576,512]{1,0:T(8,128)(2,1)} %cot_in.1, ...), custom_call_target="tpu_custom_call" | custom-call | tf_op jit(solution)/shard_map/pallas_call | solution.py:600
  86.4 2.6 %shard_map.154 = (bf16[576,512]{1,0:T(8,128)(2,1)}, f32[16,1536]{1,0:T(8,128)}, f32[16,512]{1,0:T(8,128)}, f32[16,1536]{1,0:T(8,128)}, f32[16,512]{1,0:T(8,128)}, /*index=5*/f32[32,1536]{1,0:T(8,128)}, f32[32,512]{1,0:T(8,128)}) custom-call(bf16[576,512]{1,0:T(8,128)(2,1)} %get-tuple-element.20.dtok_in, f32[8,4,16,128]{3,2,1,0:T(8,128)} %get-tuple-element.21.R, ...), custom_call_target="tpu_custom_call" | custom-call | tf_op jit(solution)/shard_map/pallas_call | solution.py:630

commit v3 on v2

--- a/solution.py
+++ b/solution.py
@@ -41,24 +41,28 @@
     for w in range(NW):
         sl=pl.ds(w*WT,WT)
         q=qkvc_ref[sl,0:128]; k=qkvc_ref[sl,128:256]; v=qkvc_ref[sl,256:384]; c=qkvc_ref[sl,384:512]
-        qt=q.T; kt=k.T; vt=v.T; ct=c.T
+        kt=k.T; vt=v.T
         cts=[];dqs=[]
         dv=jnp.zeros((WT,128),f32); dk=jnp.zeros((WT,128),f32)
+        z=jnp.zeros((),bf16)
+        lo=lane<64
+        def two(a): return jnp.concatenate([jnp.where(lo,a,z),jnp.where(lo,z,a)],0)
+        s2=dnt(two(k),q); d2=dnt(two(v),c)
+        ps=[];dss=[]
         for h in range(2):
-            m=(lane<64) if h==0 else (lane>=64)
-            z=jnp.zeros((),bf16)
-            s=dot(jnp.where(m,k,z),qt)
+            s=s2[WT*h:WT*h+WT]
             mx=jnp.max(s,axis=0,keepdims=True)
             e=jnp.exp2((s-mx)*(0.125*LOG2E))
             wt=e*(1.0/jnp.sum(e,axis=0,keepdims=True))
             p=wt.astype(bf16)
-            cts.append(dot(vt[64*h:64*h+64],p))
-            dp=dot(jnp.where(m,v,z),ct).astype(bf16).astype(f32)
+            dp=d2[WT*h:WT*h+WT].astype(bf16).astype(f32)
             t=wt*dp
             ds=(t-wt*jnp.sum(t,axis=0,keepdims=True)).astype(bf16)
-            dv=dv+dot(p,jnp.where(m,c,z))
-            dk=dk+dot(ds,jnp.where(m,q,z))
+            ps.append(p);dss.append(ds)
+            cts.append(dot(vt[64*h:64*h+64],p))
             dqs.append(dot(kt[64*h:64*h+64],ds))
+        dv=jnp.where(lo,dot(ps[0],c),dot(ps[1],c))
+        dk=jnp.where(lo,dot(dss[0],q),dot(dss[1],q))
         ctx=jnp.concatenate(cts,0).astype(bf16)
         go=go+dot(ctx,back_ref[sl,:])
         dq=(jnp.concatenate(dqs,0)*0.125).astype(bf16).T
@@ -142,7 +146,7 @@
     order_ref, tok_ref, cot_ref, gain_ref, w_ref, wo_ref, errq_ref, erro_ref, qq_ref, qo_ref, in_sem,
     W, WO, back, n, nt, xh, rstd, d, dn, qkvc,
     gbuf, xr, xm, zs, zr, gobuf, xro, xmo, zso, zro,
-    lr, mb, mr, t1, ex, ez,
+    lr, mb, mr, t1, ex, ez, S, bqi, boi,
     az_s, az_r, ax_s, ax_r, ay_s, ay_r, ac_s, ac_r,
     rx_s, rx_r, rz_s, rz_r, ro_s,
     l_s, l_r, e_s, e_r,
@@ -190,7 +194,7 @@
         front_window(w, order_ref, tok_ref, cot_ref, gain_ref, back, n, xh, rstd)
 
     source = (x // 2) == c
-    for cc in loads[:6]:
+    for cc in loads[:2]:
         cc.wait()
 
     own = y % 2
@@ -207,7 +211,6 @@
         def _():
             WO[z, x] = wo_ref[...]
 
-    fr(0)
     pl.semaphore_wait(barrier, 17)
 
     def w_z(i, k, at):
@@ -247,6 +250,9 @@
                     for k in range(1, 8):
                         wo_z(k, z).start()
 
+    for cc in loads[2:6]:
+        cc.wait()
+    fr(0)
     fr(1)
     fr(2)
 
@@ -396,14 +402,20 @@
 
     lax.fori_loop(0, 4, step, 0)
 
-    tail_norm(dn, xh, rstd, gain_ref, back, qkvc)
     merge(3)
     second(2)
+    second(3)
+    tail_norm(dn, xh, rstd, gain_ref, back, qkvc)
     tail_put(order_ref, qkvc, dtok_ref)
-    second(3)
 
     for cc in loads[6:]:
         cc.wait()
+    q = qq_ref[...].astype(f32).astype(bf16)
+    zero = jnp.zeros((32, 1536), bf16)
+    bqi[...] = jnp.concatenate([q, zero, q, zero], 0)
+    q = qo_ref[...].astype(f32).astype(bf16)
+    zero = jnp.zeros((32, 512), bf16)
+    boi[...] = jnp.concatenate([zero, q, zero, q], 0)
 
     def collect(s, carry):
         hp = hp_of(s)
@@ -427,27 +439,22 @@
 
     mqv = mq[...]
     mov = mo[...]
+    def m_copy(k):
+        return remote(mb.at[(r + k) % 8], mr.at[k - 1], l_s.at[1, k - 1], l_r.at[1, k - 1], rp(k))
+
+    def l_copy(k, at):
+        return remote(lr.at[at], lr.at[at], l_s.at[0, k - 1], l_r.at[0, k - 1], rp(k))
+
+    part = dnt(split3(mqv), bqi[...]) + dnt(split3(mov), boi[...])
+    lr[r] = ((part[0:16] + part[16:32]) + part[32:48]) * (1.0 / 127.0)
+    for k in range(1, 8):
+        l_copy(k, r).start()
     for k in range(12):
         mb[k // 2, k % 2] = mqv[:, 128 * k : 128 * k + 128]
     for k in range(4):
         mb[6 + k // 2, k % 2] = mov[:, 128 * k : 128 * k + 128]
-
-    def m_copy(k):
-        return remote(mb.at[(r + k) % 8], mr.at[k - 1], l_s.at[1, k - 1], l_r.at[1, k - 1], rp(k))
-
-    def l_copy(k, at):
-        return remote(lr.at[at], lr.at[at], l_s.at[0, k - 1], l_r.at[0, k - 1], rp(k))
-
     for k in range(1, 8):
         m_copy(k).start()
-    bqi = jnp.concatenate([qq_ref[...].astype(f32), jnp.zeros((96, 1536), f32)], 0).astype(bf16)
-    boi = jnp.concatenate(
-        [jnp.zeros((32, 512), f32), qo_ref[...].astype(f32), jnp.zeros((64, 512), f32)], 0
-    ).astype(bf16)
-    part = dnt(split3(mqv), bqi) + dnt(split3(mov), boi)
-    lr[r] = ((part[0:16] + part[16:32]) + part[32:48]) * (1.0 / 127.0)
-    for k in range(1, 8):
-        l_copy(k, r).start()
     for k in range(1, 8):
         m_copy(k).wait_recv()
     total = mb[r]
@@ -462,16 +469,19 @@
     left_ref[...] = left
 
     lt = left.T
-    lane = lax.broadcasted_iota(jnp.int32, (32, 128), 1)
+    lane = lax.broadcasted_iota(jnp.int32, (16, 128), 1)
     full = hdot(lt, left)
-    gram = jnp.where(lane < 32, full[0:32], jnp.where(lane < 64, full[32:64], 0.0))
+    gram = jnp.where(
+        lane < 64,
+        jnp.where(lane < 32, full[0:16], full[32:48]),
+        jnp.where(lane < 96, full[16:32], full[48:64]),
+    )
     mine = jnp.where(r < 6, lt[0:32], lt[32:64])
     for j in range(2):
         t = hdot(mine, total[j])
-        t1[2 * j, 0:16] = t[0:16]
-        t1[2 * j + 1, 0:16] = t[16:32]
-    for k in range(4):
-        t1[k, 16:48] = gram
+        for k in range(2):
+            t1[2 * j + k, 0:16] = t[16 * k : 16 * k + 16]
+            t1[2 * j + k, 16:24] = gram[8 * k : 8 * k + 8]
     ex[x] = t1[x]
 
     def e_x(k, to, at):
@@ -481,7 +491,7 @@
         return remote(ez.at[at], ez.at[at], e_s.at[1, k - 1], e_r.at[1, k - 1], zp(k))
 
     def a_x(k, at):
-        return remote(R.at[r, at], R.at[r, at], e_s.at[2, k - 1], e_r.at[2, k - 1], xp(k))
+        return remote(S.at[at], S.at[at], e_s.at[2, k - 1], e_r.at[2, k - 1], xp(k))
 
     def a_r(k, at):
         return remote(R.at[at], R.at[at], e_s.at[3, k - 1], e_r.at[3, k - 1], rp(k))
@@ -498,16 +508,18 @@
     total = ez[0]
     for k in range(1, 8):
         total = total + ez[k]
-    R[r, x] = total[0:16]
+    S[x] = total
     for k in range(1, 4):
         a_x(k, x).start()
-    iq, io = inverse_factors(total[16:48])
+    for k in range(1, 4):
+        a_x(k, (x - k + 4) % 4).wait_recv()
+    R[r] = S[:, 0:16]
+    for k in range(1, 8):
+        a_r(k, r).start()
+    gram = jnp.concatenate([S[0, 16:24], S[1, 16:24]], 0)
+    iq, io = inverse_factors(jnp.concatenate([gram, pltpu.roll(gram, 64, 1)], 0))
     inv_ref[0] = iq
     inv_ref[1] = io
-    for k in range(1, 4):
-        a_x(k, (x - k + 4) % 4).wait_recv()
-    for k in range(1, 8):
-        a_r(k, r).start()
     for k in range(1, 8):
         a_r(k, (r - k + 8) % 8).wait_recv()
 
@@ -615,7 +627,8 @@
             V((4, 8, 4, 16, 384), bf16), V((3, 4, 2, 4, 16, 384), bf16), V((4, 2, 4, 16, 384), bf16), V((4, 8, 16, 384), bf16), V((4, 7, 16, 384), bf16),
             V((4, 2, 4, 16, 512), bf16), V((3, 4, 2, 16, 512), bf16), V((4, 2, 16, 512), bf16), V((4, 2, 16, 512), bf16), V((7, 16, 512), bf16),
             V((8, 16, 128), f32), V((8, 2, 16, 128), f32), V((7, 2, 16, 128), f32),
-            V((4, 48, 128), f32), V((4, 48, 128), f32), V((8, 48, 128), f32),
+            V((4, 24, 128), f32), V((4, 24, 128), f32), V((8, 24, 128), f32), V((4, 24, 128), f32),
+            V((128, 1536), bf16), V((128, 512), bf16),
             dma((3, 7)), dma((3, 7)), dma((2, 2, 3)), dma((2, 2, 3)), dma((2, 2)), dma((2, 2)), dma((2, 4)), dma((2, 4)),
             dma((2, 3, 4, 2)), dma((2, 3, 4, 2)), dma((1, 4, 7)), dma((2, 4, 7)), dma((4, 2)),
             dma((2, 7)), dma((2, 7)), dma((4, 7)), dma((4, 7)),

time: 89.1 us -> 83.8 us (0.941)
  Pallas kernels: 88.3 us -> 83 us
    pallas_call x1, Pallas kernels: 85.7 us -> 80.5 us  [per_device(): pl.pallas_call(functools.partial(kernel, scale), out_shape=(shape((576, 5...]
where the time goes in v3:
time: 83.8 us; the launch traced here: 83.7 us
  Pallas kernels  83 us (99%)
    pallas_call x1, Pallas kernels, per_device(): pl.pallas_call(functools.partial(kernel, scale), out_shape=(shape((576, 5...  80.5 us
    pallas_call x1, Pallas kernels, per_device(): pl.pallas_call(finish, out_shape=(shape((576, 512), bf16), shape((16, 153...  2.56 us

profile of v3, /device:TPU:1, one launch (start us, length us, event | category | flops | bytes accessed | tf_op | source)
XLA Modules:
  0.0 83.7 jit_solution(17115754968508553641)
XLA Ops:
  0.6 80.5 %shard_map.153 = (bf16[576,512]{1,0:T(8,128)(2,1)}, f32[8,4,16,128]{3,2,1,0:T(8,128)}, f32[16,128]{1,0:T(8,128)}, f32[2,32,32]{2,1,0:T(8,128)}, f32[16,1536]{1,0:T(8,128)}, /*index=5*/f32[16,512]{1,0:T(8,128)}) custom-call(s32[1,576]{1,0:T(1,128)} %order_in.1, bf16[576,512]{1,0:T(8,128)(2,1)} %tok_in.1, bf16[576,512]{1,0:T(8,128)(2,1)} %cot_in.1, ...), custom_call_target="tpu_custom_call" | custom-call | tf_op jit(solution)/shard_map/pallas_call | solution.py:612
  81.1 2.6 %shard_map.154 = (bf16[576,512]{1,0:T(8,128)(2,1)}, f32[16,1536]{1,0:T(8,128)}, f32[16,512]{1,0:T(8,128)}, f32[16,1536]{1,0:T(8,128)}, f32[16,512]{1,0:T(8,128)}, /*index=5*/f32[32,1536]{1,0:T(8,128)}, f32[32,512]{1,0:T(8,128)}) custom-call(bf16[576,512]{1,0:T(8,128)(2,1)} %get-tuple-element.20.dtok_in, f32[8,4,16,128]{3,2,1,0:T(8,128)} %get-tuple-element.21.R, ...), custom_call_target="tpu_custom_call" | custom-call | tf_op jit(solution)/shard_map/pallas_call | solution.py:643

commit v4 on v3

--- a/solution.py
+++ b/solution.py
@@ -38,37 +38,46 @@
     if mid is not None: mid()
     lane=lax.broadcasted_iota(jnp.int32,(WT,128),1)
     go=jnp.zeros((128,512),f32)
-    for w in range(NW):
-        sl=pl.ds(w*WT,WT)
-        q=qkvc_ref[sl,0:128]; k=qkvc_ref[sl,128:256]; v=qkvc_ref[sl,256:384]; c=qkvc_ref[sl,384:512]
-        kt=k.T; vt=v.T
-        cts=[];dqs=[]
-        dv=jnp.zeros((WT,128),f32); dk=jnp.zeros((WT,128),f32)
-        z=jnp.zeros((),bf16)
-        lo=lane<64
-        def two(a): return jnp.concatenate([jnp.where(lo,a,z),jnp.where(lo,z,a)],0)
-        s2=dnt(two(k),q); d2=dnt(two(v),c)
-        ps=[];dss=[]
-        for h in range(2):
-            s=s2[WT*h:WT*h+WT]
-            mx=jnp.max(s,axis=0,keepdims=True)
-            e=jnp.exp2((s-mx)*(0.125*LOG2E))
-            wt=e*(1.0/jnp.sum(e,axis=0,keepdims=True))
-            p=wt.astype(bf16)
-            dp=d2[WT*h:WT*h+WT].astype(bf16).astype(f32)
-            t=wt*dp
-            ds=(t-wt*jnp.sum(t,axis=0,keepdims=True)).astype(bf16)
-            ps.append(p);dss.append(ds)
-            cts.append(dot(vt[64*h:64*h+64],p))
-            dqs.append(dot(kt[64*h:64*h+64],ds))
-        dv=jnp.where(lo,dot(ps[0],c),dot(ps[1],c))
-        dk=jnp.where(lo,dot(dss[0],q),dot(dss[1],q))
-        ctx=jnp.concatenate(cts,0).astype(bf16)
-        go=go+dot(ctx,back_ref[sl,:])
-        dq=(jnp.concatenate(dqs,0)*0.125).astype(bf16).T
-        d_ref[sl,0:128]=dq
-        d_ref[sl,128:256]=(dk*0.125).astype(bf16)
-        d_ref[sl,256:384]=dv.astype(bf16)
+    z=jnp.zeros((),bf16)
+    lo=lane<64
+    def two(a): return jnp.concatenate([jnp.where(lo,a,z),jnp.where(lo,z,a)],0)
+    for w0 in range(0,NW,4):
+        ws=range(w0,w0+4)
+        sd={}
+        for w in ws:
+            sl=pl.ds(w*WT,WT)
+            q=qkvc_ref[sl,0:128]; k=qkvc_ref[sl,128:256]; v=qkvc_ref[sl,256:384]; c=qkvc_ref[sl,384:512]
+            sd[w]=(dnt(two(k),q),dnt(two(v),c))
+        pd={}
+        for w in ws:
+            s2,d2=sd[w]
+            ps=[];dss=[]
+            for h in range(2):
+                s=s2[WT*h:WT*h+WT]
+                mx=jnp.max(s,axis=0,keepdims=True)
+                e=jnp.exp2((s-mx)*(0.125*LOG2E))
+                wt=e*(1.0/jnp.sum(e,axis=0,keepdims=True))
+                p=wt.astype(bf16)
+                dp=d2[WT*h:WT*h+WT].astype(bf16).astype(f32)
+                t=wt*dp
+                ds=(t-wt*jnp.sum(t,axis=0,keepdims=True)).astype(bf16)
+                ps.append(p);dss.append(ds)
+            pd[w]=(ps,dss)
+        for w in ws:
+            sl=pl.ds(w*WT,WT)
+            ps,dss=pd[w]
+            q=qkvc_ref[sl,0:128]; k=qkvc_ref[sl,128:256]; v=qkvc_ref[sl,256:384]; c=qkvc_ref[sl,384:512]
+            kt=k.T; vt=v.T
+            cts=[dot(vt[:64],ps[0]),dot(vt[64:],ps[1])]
+            dqs=[dot(kt[:64],dss[0]),dot(kt[64:],dss[1])]
+            dv=jnp.where(lo,dot(ps[0],c),dot(ps[1],c))
+            dk=jnp.where(lo,dot(dss[0],q),dot(dss[1],q))
+            ctx=jnp.concatenate(cts,0).astype(bf16)
+            go=go+dot(ctx,back_ref[sl,:])
+            dq=(jnp.concatenate(dqs,0)*0.125).astype(bf16).T
+            d_ref[sl,0:128]=dq
+            d_ref[sl,128:256]=(dk*0.125).astype(bf16)
+            d_ref[sl,256:384]=dv.astype(bf16)
     go_store((go*scale).astype(bf16))
     g_store((dot(nt_ref[...],d_ref[...])*scale).astype(bf16))
     dn=dnt(d_ref[...],W)
@@ -288,12 +297,14 @@
         )
 
     def y_copy(i, hp):
-        a, b = half(hp, c)
-        to = yp((1 + 2 * own + 2 * i) % 4)
-        return (
-            remote(a, a, ay_s.at[0, i], ay_r.at[0, i], to),
-            remote(b, b, ay_s.at[1, i], ay_r.at[1, i], to),
-        )
+        out = []
+        for way in range(2):
+            a = W.at[hp, pl.ds(4 * way, 4), pl.ds(2 * c, 2)]
+            b = WO.at[pl.ds(2 * hp + way, 1), pl.ds(2 * c, 2)]
+            to = yp(1 + 2 * way)
+            out.append(remote(a, a, ay_s.at[0, i, way], ay_r.at[0, i, way], to))
+            out.append(remote(b, b, ay_s.at[1, i, way], ay_r.at[1, i, way], to))
+        return out
 
     def spread(i):
         wait_x(i)
@@ -629,7 +640,7 @@
             V((8, 16, 128), f32), V((8, 2, 16, 128), f32), V((7, 2, 16, 128), f32),
             V((4, 24, 128), f32), V((4, 24, 128), f32), V((8, 24, 128), f32), V((4, 24, 128), f32),
             V((128, 1536), bf16), V((128, 512), bf16),
-            dma((3, 7)), dma((3, 7)), dma((2, 2, 3)), dma((2, 2, 3)), dma((2, 2)), dma((2, 2)), dma((2, 4)), dma((2, 4)),
+            dma((3, 7)), dma((3, 7)), dma((2, 2, 3)), dma((2, 2, 3)), dma((2, 2, 2)), dma((2, 2, 2)), dma((2, 4)), dma((2, 4)),
             dma((2, 3, 4, 2)), dma((2, 3, 4, 2)), dma((1, 4, 7)), dma((2, 4, 7)), dma((4, 2)),
             dma((2, 7)), dma((2, 7)), dma((4, 7)), dma((4, 7)),
         ],

time: 83.8 us -> 82.8 us (0.988)
  Pallas kernels: 83 us -> 82 us
    pallas_call x1, Pallas kernels: 80.5 us -> 79.4 us  [per_device(): pl.pallas_call(functools.partial(kernel, scale), out_shape=(shape((576, 5...]
where the time goes in v4:
time: 82.8 us; the launch traced here: 82.6 us
  Pallas kernels  82 us (99%)
    pallas_call x1, Pallas kernels, per_device(): pl.pallas_call(functools.partial(kernel, scale), out_shape=(shape((576, 5...  79.4 us
    pallas_call x1, Pallas kernels, per_device(): pl.pallas_call(finish, out_shape=(shape((576, 512), bf16), shape((16, 153...  2.57 us

profile of v4, /device:TPU:1, one launch (start us, length us, event | category | flops | bytes accessed | tf_op | source)
XLA Modules:
  0.0 82.6 jit_solution(11301551902588998469)
XLA Ops:
  0.6 79.4 %shard_map.153 = (bf16[576,512]{1,0:T(8,128)(2,1)}, f32[8,4,16,128]{3,2,1,0:T(8,128)}, f32[16,128]{1,0:T(8,128)}, f32[2,32,32]{2,1,0:T(8,128)}, f32[16,1536]{1,0:T(8,128)}, /*index=5*/f32[16,512]{1,0:T(8,128)}) custom-call(s32[1,576]{1,0:T(1,128)} %order_in.1, bf16[576,512]{1,0:T(8,128)(2,1)} %tok_in.1, bf16[576,512]{1,0:T(8,128)(2,1)} %cot_in.1, ...), custom_call_target="tpu_custom_call" | custom-call | tf_op jit(solution)/shard_map/pallas_call | solution.py:623
  80.1 2.6 %shard_map.154 = (bf16[576,512]{1,0:T(8,128)(2,1)}, f32[16,1536]{1,0:T(8,128)}, f32[16,512]{1,0:T(8,128)}, f32[16,1536]{1,0:T(8,128)}, f32[16,512]{1,0:T(8,128)}, /*index=5*/f32[32,1536]{1,0:T(8,128)}, f32[32,512]{1,0:T(8,128)}) custom-call(bf16[576,512]{1,0:T(8,128)(2,1)} %get-tuple-element.20.dtok_in, f32[8,4,16,128]{3,2,1,0:T(8,128)} %get-tuple-element.21.R, ...), custom_call_target="tpu_custom_call" | custom-call | tf_op jit(solution)/shard_map/pallas_call | solution.py:654

commit v5 on v4

--- a/solution.py
+++ b/solution.py
@@ -10,6 +10,7 @@
 f32 = jnp.float32
 bf16 = jnp.bfloat16
 MESH = pl.DeviceIdType.MESH
+FAR = (4, 3, 5, 2, 6, 1, 7)
 def dot(a,b): return jnp.dot(a,b,preferred_element_type=f32)
 def dnt(a,b): return lax.dot_general(a,b,(((1,),(1,)),((),())),preferred_element_type=f32)
 WT=144; NW=4
@@ -250,7 +251,7 @@
     @pl.when(source)
     def _():
         for i in range(2):
-            for k in range(1, 8):
+            for k in FAR:
                 w_z(i, k, z).start()
             if i == 0:
 
@@ -365,7 +366,7 @@
             zs[s, rows] = total.astype(bf16)
             total = gobuf[s, h, x].astype(f32) + (xro[1, s, 1 - h].astype(f32) + xro[2, s, h].astype(f32))
             zso[s, h] = total.astype(bf16)
-        for k in range(1, 8):
+        for k in FAR:
             z_send(s, k).start()
         zo_each(s, lambda cc: cc.start())
 
@@ -457,14 +458,16 @@
         return remote(lr.at[at], lr.at[at], l_s.at[0, k - 1], l_r.at[0, k - 1], rp(k))
 
     part = dnt(split3(mqv), bqi[...]) + dnt(split3(mov), boi[...])
-    lr[r] = ((part[0:16] + part[16:32]) + part[32:48]) * (1.0 / 127.0)
-    for k in range(1, 8):
+    part = ((part[0:16] + part[16:32]) + part[32:48]) * (1.0 / 127.0)
+    low = lax.broadcasted_iota(jnp.int32, (8, 128), 1) < 64
+    lr[r] = jnp.where(low, part[0:8], part[8:16])
+    for k in FAR:
         l_copy(k, r).start()
     for k in range(12):
         mb[k // 2, k % 2] = mqv[:, 128 * k : 128 * k + 128]
     for k in range(4):
         mb[6 + k // 2, k % 2] = mov[:, 128 * k : 128 * k + 128]
-    for k in range(1, 8):
+    for k in FAR:
         m_copy(k).start()
     for k in range(1, 8):
         m_copy(k).wait_recv()
@@ -477,6 +480,8 @@
     for k in range(1, 8):
         left = left + lr[k]
     left = left * 0.125
+    turned = pltpu.roll(left, 64, 1)
+    left = jnp.concatenate([jnp.where(low, left, turned), jnp.where(low, turned, left)], 0)
     left_ref[...] = left
 
     lt = left.T
@@ -507,12 +512,12 @@
     def a_r(k, at):
         return remote(R.at[at], R.at[at], e_s.at[3, k - 1], e_r.at[3, k - 1], rp(k))
 
-    for k in range(1, 4):
+    for k in (2, 1, 3):
         e_x(k, (x + k) % 4, x).start()
     for k in range(1, 4):
         e_x(k, x, (x - k + 4) % 4).wait_recv()
     ez[z] = (ex[0] + ex[1]) + (ex[2] + ex[3])
-    for k in range(1, 8):
+    for k in FAR:
         e_z(k, z).start()
     for k in range(1, 8):
         e_z(k, (z - k + 8) % 8).wait_recv()
@@ -520,12 +525,12 @@
     for k in range(1, 8):
         total = total + ez[k]
     S[x] = total
-    for k in range(1, 4):
+    for k in (2, 1, 3):
         a_x(k, x).start()
     for k in range(1, 4):
         a_x(k, (x - k + 4) % 4).wait_recv()
     R[r] = S[:, 0:16]
-    for k in range(1, 8):
+    for k in FAR:
         a_r(k, r).start()
     gram = jnp.concatenate([S[0, 16:24], S[1, 16:24]], 0)
     iq, io = inverse_factors(jnp.concatenate([gram, pltpu.roll(gram, 64, 1)], 0))
@@ -637,7 +642,7 @@
             V((576, 512), f32), V((576, 1), f32), V((576, 384), bf16), V((576, 512), f32), V((576, 512), bf16),
             V((4, 8, 4, 16, 384), bf16), V((3, 4, 2, 4, 16, 384), bf16), V((4, 2, 4, 16, 384), bf16), V((4, 8, 16, 384), bf16), V((4, 7, 16, 384), bf16),
             V((4, 2, 4, 16, 512), bf16), V((3, 4, 2, 16, 512), bf16), V((4, 2, 16, 512), bf16), V((4, 2, 16, 512), bf16), V((7, 16, 512), bf16),
-            V((8, 16, 128), f32), V((8, 2, 16, 128), f32), V((7, 2, 16, 128), f32),
+            V((8, 8, 128), f32), V((8, 2, 16, 128), f32), V((7, 2, 16, 128), f32),
             V((4, 24, 128), f32), V((4, 24, 128), f32), V((8, 24, 128), f32), V((4, 24, 128), f32),
             V((128, 1536), bf16), V((128, 512), bf16),
             dma((3, 7)), dma((3, 7)), dma((2, 2, 3)), dma((2, 2, 3)), dma((2, 2, 2)), dma((2, 2, 2)), dma((2, 4)), dma((2, 4)),

time: 82.8 us -> 81.2 us (0.981)
  Pallas kernels: 82 us -> 80.4 us
    pallas_call x1, Pallas kernels: 79.4 us -> 77.8 us  [per_device(): pl.pallas_call(functools.partial(kernel, scale), out_shape=(shape((576, 5...]
where the time goes in v5:
time: 81.2 us; the launch traced here: 81 us
  Pallas kernels  80.4 us (99%)
    pallas_call x1, Pallas kernels, per_device(): pl.pallas_call(functools.partial(kernel, scale), out_shape=(shape((576, 5...  77.8 us
    pallas_call x1, Pallas kernels, per_device(): pl.pallas_call(finish, out_shape=(shape((576, 512), bf16), shape((16, 153...  2.56 us

profile of v5, /device:TPU:1, one launch (start us, length us, event | category | flops | bytes accessed | tf_op | source)
XLA Modules:
  0.0 81.0 jit_solution(14497956160298701787)
XLA Ops:
  0.6 77.8 %shard_map.153 = (bf16[576,512]{1,0:T(8,128)(2,1)}, f32[8,4,16,128]{3,2,1,0:T(8,128)}, f32[16,128]{1,0:T(8,128)}, f32[2,32,32]{2,1,0:T(8,128)}, f32[16,1536]{1,0:T(8,128)}, /*index=5*/f32[16,512]{1,0:T(8,128)}) custom-call(s32[1,576]{1,0:T(1,128)} %order_in.1, bf16[576,512]{1,0:T(8,128)(2,1)} %tok_in.1, bf16[576,512]{1,0:T(8,128)(2,1)} %cot_in.1, ...), custom_call_target="tpu_custom_call" | custom-call | tf_op jit(solution)/shard_map/pallas_call | solution.py:628
  78.5 2.6 %shard_map.154 = (bf16[576,512]{1,0:T(8,128)(2,1)}, f32[16,1536]{1,0:T(8,128)}, f32[16,512]{1,0:T(8,128)}, f32[16,1536]{1,0:T(8,128)}, f32[16,512]{1,0:T(8,128)}, /*index=5*/f32[32,1536]{1,0:T(8,128)}, f32[32,512]{1,0:T(8,128)}) custom-call(bf16[576,512]{1,0:T(8,128)(2,1)} %get-tuple-element.20.dtok_in, f32[8,4,16,128]{3,2,1,0:T(8,128)} %get-tuple-element.21.R, ...), custom_call_target="tpu_custom_call" | custom-call | tf_op jit(solution)/shard_map/pallas_call | solution.py:659
